TPU v7x, 32 devices: a whole 2x2x4 slice. The times are simulated.
32 devices in a mesh: grp: 2 (over y), tile: 4 (over z), date: 2 (over x), row: 2 (over core).
Axes of the slice: x: 2, y: 2, z: 4, core: 2. Of those that a mesh axis runs over, the one named last changes fastest.
Arguments:
- images: bfloat16 [16, 10, 64, 1024], P('date', None, ('grp', 'tile', 'row')), parts along dimension 2, may hold values from -6 to 6
- clouds: int32 [16, 32, 512], P('date', ('grp', 'tile', 'row')), parts along dimension 1, may hold values from 0 to 1, as said below
- day_of_year: int32 [32], P(('grp', 'date')), parts along dimension 0, may hold values from 0 to 365
- conv_first: bfloat16 [9, 64, 10], replicated, may hold values from -0.625 to 0.625
- conv_second: bfloat16 [9, 64, 64], replicated, may hold values from -0.25 to 0.25
- conv_down: bfloat16 [4, 128, 64], replicated, may hold values from -0.375 to 0.375
- conv_coarse: bfloat16 [9, 128, 128], replicated, may hold values from -0.1875 to 0.1875
- key_weight: bfloat16 [64, 128], replicated, may hold values from -0.5 to 0.5
- query_weight: float32 [16, 4], replicated
- out_weight: bfloat16 [128, 128], replicated, may hold values from -0.5 to 0.5
- up_weight: bfloat16 [4, 64, 128], replicated, may hold values from -0.5 to 0.5
- dec_weight: bfloat16 [9, 64, 128], replicated, may hold values from -0.1875 to 0.1875
- cls_weight: bfloat16 [20, 64], replicated, may hold values from -0.75 to 0.75
- cls_bias: float32 [20], replicated, may hold values from -4 to 4
Outputs:
- logits: float32 [20, 64, 1024], P(None, ('grp', 'tile', 'row'), 'date'), parts along dimension 1
There are 2 independent parts, one for each index of `grp`. A program takes and returns all parts, laid end to end along the dimension named above; an argument that names none is the same for every part. Nothing has to cross between parts.
Inputs may be any that keep to these rules, and one draw needn't show every extreme that they name: `clouds`: every pixel of the half-resolution grid has at least one date with value 1.
All inputs are finite; a program needn't handle non-finite values.
Results may differ from a plain program's by a relative error of at most 0.008.
Values may be sent and summed in bfloat16 or wider, within the bound.
A program may use at most 192 MiB of HBM per device.

v0:
```python
import jax
import jax.numpy as jnp
from jax import lax
from jax.sharding import PartitionSpec as P


def extended_2(block, sides, width):
    for axis, dim in sides:
        count = lax.axis_size(axis)
        forward = [(i, i + 1) for i in range(count - 1)]
        backward = [(target, source) for source, target in forward]
        low = lax.ppermute(
            lax.slice_in_dim(block, block.shape[dim] - width, None, axis=dim), axis, forward
        )
        high = lax.ppermute(lax.slice_in_dim(block, 0, width, axis=dim), axis, backward)
        block = jnp.concatenate([low, block, high], axis=dim)
    return block


def combined_all(value, axis, join):
    pieces = jax.tree.map(lambda part: lax.all_gather(part, axis), value)
    head = jax.tree.map(lambda part: part[0], pieces)
    tail = jax.tree.map(lambda part: part[1:], pieces)
    total, _ = lax.scan(lambda total, section: (join(total, section), None), head, tail)
    return total


def rms_norm(values, axis):
    return values * lax.rsqrt(jnp.mean(values * values, axis=axis, keepdims=True) + 1e-05)


def activate(values, axis):
    return jnp.maximum(rms_norm(values, axis), 0.0)


def conv_valid(padded, weight):
    row_count = padded.shape[-2] - 2
    col_count = padded.shape[-1] - 2
    result = None
    for tap_index in range(9):
        tap_row = tap_index // 3
        tap_col = tap_index % 3
        window = padded[..., tap_row : tap_row + row_count, tap_col : tap_col + col_count]
        term_map = jnp.einsum(
            "oi,...iyx->...oyx", weight[tap_index], window, preferred_element_type=jnp.float32
        )
        result = term_map if result is None else result + term_map
    return result


def section(extended, weight):
    return activate(conv_valid(extended, weight), 1).astype(jnp.bfloat16)


def pad_cols(values):
    return jnp.pad(values, [(0, 0)] * (values.ndim - 1) + [(1, 1)])


def lower_maps(fine_map, conv_down):
    date_local, fine_ch, row_count, col_count = fine_map.shape
    coarse_ch = conv_down.shape[1]
    blocks = fine_map.reshape(date_local, fine_ch, row_count // 2, 2, col_count // 2, 2)
    lowered = jnp.einsum(
        "abou,nuyaxb->noyx",
        conv_down.reshape(2, 2, coarse_ch, fine_ch),
        blocks,
        preferred_element_type=jnp.float32,
    )
    return activate(lowered, 1).astype(jnp.bfloat16)


def upsample(coarse_out, up_weight):
    channels = up_weight.shape[1]
    row_count = coarse_out.shape[1]
    col_count = coarse_out.shape[2]
    taps = jnp.einsum("koi,iyx->koyx", up_weight, coarse_out, preferred_element_type=jnp.float32)
    taps = taps.reshape(2, 2, channels, row_count, col_count).transpose(2, 3, 0, 4, 1)
    return taps.reshape(channels, 2 * row_count, 2 * col_count).astype(jnp.bfloat16)


def classify(extended, dec_weight, cls_weight, cls_bias):
    decoded = activate(conv_valid(extended, dec_weight), 0).astype(jnp.bfloat16)
    scores_out = jnp.einsum("co,oyx->cyx", cls_weight, decoded, preferred_element_type=jnp.float32)
    return scores_out + cls_bias[:, None, None]


def combine_parts(earlier, later):
    max_one, total_one, sum_one = earlier
    max_two, total_two, sum_two = later
    top = jnp.maximum(max_one, max_two)
    factor_one = jnp.exp(max_one - top)
    factor_two = jnp.exp(max_two - top)
    return (
        top,
        total_one * factor_one + total_two * factor_two,
        sum_one * factor_one[:, None] + sum_two * factor_two[:, None],
    )


def body(
    images,
    clouds,
    day_of_year,
    conv_first,
    conv_second,
    conv_down,
    conv_coarse,
    key_weight,
    query_weight,
    out_weight,
    up_weight,
    dec_weight,
    cls_weight,
    cls_bias,
):
    date_local = images.shape[0]
    full_cols = images.shape[3]
    fine_ch = conv_second.shape[1]
    coarse_ch = conv_coarse.shape[1]
    head_count = query_weight.shape[0]
    key_size = query_weight.shape[1]
    date_count = lax.axis_size("date")
    date_index = lax.axis_index("date")
    share = full_cols // date_count
    extended = extended_2(images, ((("tile", "row"), 2),), 1)
    first_map = section(pad_cols(extended), conv_first)
    first_ext = extended_2(first_map, ((("tile", "row"), 2),), 1)
    fine_map = section(pad_cols(first_ext), conv_second)
    lowered = lower_maps(fine_map, conv_down)
    lowered_ext = extended_2(lowered, ((("tile", "row"), 2),), 1)
    coarse_map = section(pad_cols(lowered_ext), conv_coarse)
    row_count = fine_map.shape[2]
    col_count = fine_map.shape[3]
    coarse_rows = row_count // 2
    coarse_cols = col_count // 2
    half_ch = coarse_ch // 2
    freqs = jnp.power(1000.0, -2.0 * jnp.arange(half_ch, dtype=jnp.float32) / coarse_ch)
    angles = day_of_year.astype(jnp.float32)[:, None] * freqs[None, :]
    encoding = jnp.concatenate([jnp.sin(angles), jnp.cos(angles)], axis=1)
    key_maps = jnp.einsum(
        "ko,nohw->nkhw", key_weight, coarse_map, preferred_element_type=jnp.float32
    )
    key_maps = (
        key_maps
        + jnp.dot(encoding, key_weight.astype(jnp.float32).T, precision=lax.Precision.HIGHEST)[
            :, :, None, None
        ]
    )
    key_maps = key_maps.reshape(date_local, head_count, key_size, coarse_rows, coarse_cols)
    scores = 0.5 * jnp.sum(key_maps * query_weight[None, :, :, None, None], axis=2)
    is_valid = (clouds == 1)[:, None]
    masked = jnp.where(is_valid, scores, -1e30)
    local_max = jnp.max(masked, axis=0)
    expd = jnp.where(is_valid, jnp.exp(masked - local_max[None]), 0.0)
    local_total = jnp.sum(expd, axis=0)
    grouped = coarse_map.astype(jnp.float32).reshape(
        date_local, head_count, coarse_ch // head_count, coarse_rows, coarse_cols
    )
    local_sum = jnp.sum(expd[:, :, None] * grouped, axis=0)
    glob_max, glob_total, glob_sum = combined_all(
        (local_max, local_total, local_sum), "date", combine_parts
    )
    aggregate = (
        (glob_sum / glob_total[:, None])
        .reshape(coarse_ch, coarse_rows, coarse_cols)
        .astype(jnp.bfloat16)
    )
    coarse_out = activate(
        jnp.einsum("oi,ihw->ohw", out_weight, aggregate, preferred_element_type=jnp.float32), 0
    ).astype(jnp.bfloat16)
    attention = jnp.where(is_valid, jnp.exp(masked - glob_max[None]), 0.0) / glob_total[None]
    attn_fine = jnp.repeat(jnp.repeat(attention, 2, axis=2), 2, axis=3)
    fine_group = fine_map.astype(jnp.float32).reshape(
        date_local, head_count, fine_ch // head_count, row_count, col_count
    )
    partial_value = jnp.sum(attn_fine[:, :, None] * fine_group, axis=0).reshape(
        fine_ch, row_count, col_count
    )
    skip_map = lax.psum(partial_value.astype(jnp.bfloat16), "date")
    up_map = upsample(coarse_out, up_weight)
    joined = jnp.concatenate([up_map, skip_map], axis=0)
    joined_rows = extended_2(joined, ((("tile", "row"), 1),), 1)
    joined_ext = lax.dynamic_slice_in_dim(pad_cols(joined_rows), date_index * share, share + 2, 2)
    return classify(joined_ext, dec_weight, cls_weight, cls_bias)


def solution(mesh):
    return jax.shard_map(
        body,
        mesh=mesh,
        in_specs=(
            P("date", None, ("grp", "tile", "row"), None),
            P("date", ("grp", "tile", "row"), None),
            P(("grp", "date")),
            P(),
            P(),
            P(),
            P(),
            P(),
            P(),
            P(),
            P(),
            P(),
            P(),
            P(),
        ),
        out_specs=P(None, ("grp", "tile", "row"), "date"),
        check_vma=False,
    )
```

profile of v0, /device:TPU:1, one launch (start us, length us, event | category | flops | bytes accessed | tf_op | source)
XLA Modules:
  0.0 382.4 jit_solution(9848550667759250688)
XLA Ops:
  8.0 4.6 %collective-permute-start = (bf16[8,10,1,1024]{3,1,2,0:T(8,128)(2,1)S(1)}, bf16[8,10,1,1024]{3,1,2,0:T(8,128)(2,1)S(1)}, u32[]{:S(2)}, u32[]{:S(2)}) collective-permute-start(bf16[8,10,1,1024]{3,1,2,0:T(8,128)(2,1)S(1)} %get-tuple-element.39), channel_id=1, source_target_pairs={{0,1},{1,4},{4,5},{5,8},{8,9},{9,12},{12,13},{2,3},{3,6},{6,7},{7,... | collective-permute-start | bytes 491528 | tf_op jit(solution)/shard_map/ppermute | solution.py:12
  14.5 5.7 %fusion.127 = f32[8,4,1024,64]{2,3,1,0:T(8,128)} fusion(bf16[8,10,4,1024]{3,2,1,0:T(4,128)(2,1)} %param.14, bf16[9,64,10]{1,2,0:T(8,128)(2,1)} %param.17), kind=kOutput, calls=%fused_computation.171 | convolution fusion | flops 41943040 | bytes 9048064 | tf_op jit(solution)/shard_map/oi,...iyx->...oyx/dot_general | solution.py:44
  25.9 4.8 %fusion.85 = f32[8,4,1024,64]{2,3,1,0:T(8,128)} fusion(bf16[8,10,6,1026]{3,1,2,0:T(8,128)(2,1)S(1)} %fusion.69, bf16[9,64,10]{1,2,0:T(8,128)(2,1)S(1)} %copy-done.11), kind=kOutput, calls=%fused_computation.118 | convolution fusion | flops 41943040 | bytes 9441280 | tf_op jit(solution)/shard_map/oi,...iyx->...oyx/dot_general | solution.py:44
  35.2 4.8 %fusion.89 = f32[8,4,1024,64]{2,3,1,0:T(8,128)} fusion(bf16[8,10,6,1026]{3,1,2,0:T(8,128)(2,1)S(1)} %fusion.69, bf16[9,64,10]{1,2,0:T(8,128)(2,1)S(1)} %copy-done.11), kind=kOutput, calls=%fused_computation.122 | convolution fusion | flops 41943040 | bytes 9441280 | tf_op jit(solution)/shard_map/oi,...iyx->...oyx/dot_general | solution.py:44
  47.2 33.3 %multiply_reduce_fusion.1 = (f32[8,4,1024]{2,1,0:T(4,128)S(1)}, f32[8,4,1024,64]{2,3,1,0:T(8,128)}) fusion(bf16[9,64,10]{1,2,0:T(8,128)(2,1)S(1)} %copy-done.11, bf16[8,10,6,1026]{3,1,2,0:T(8,128)(2,1)} %copy-done.5, f32[8,4,1024,64]{2,3,1,0:T(8,128)S(1)} %fusion.74, f32[8,4,1024,64]{2,3,1,0:T(8,128)} %fusion.83, f32[8,4,1024,64]{2,3,1,0:T(8,128)} %fusion.85, ...), kind=kOutput, calls=%fused_computation.11 | convolution fusion | flops 62881792 | bytes 76681216 | tf_op jit(solution)/shard_map/oi,...iyx->...oyx/dot_general | solution.py:44
  80.5 4.8 %fusion.14 = bf16[8,64,4,1024]{3,1,2,0:T(8,128)(2,1)S(1)} fusion(f32[8,4,1024,64]{2,3,1,0:T(8,128)} %get-tuple-element.46, f32[8,4,1024]{2,1,0:T(4,128)S(1)} %add_rsqrt_fusion.1), kind=kLoop, calls=%fused_computation.27 | loop fusion | flops 6291456 | bytes 12713984 | tf_op jit(solution)/shard_map/convert_element_type | solution.py:52
  94.3 6.8 %fusion.162 = f32[8,4,1024,64]{2,3,1,0:T(8,128)} fusion(bf16[8,64,4,1024]{3,1,2,0:T(8,128)(2,1)} %copy-done.2, bf16[9,64,64]{2,1,0:T(8,128)(2,1)S(1)} %copy-done.8), kind=kOutput, calls=%fused_computation.214 | convolution fusion | flops 268435456 | bytes 12599296 | tf_op jit(solution)/shard_map/oi,...iyx->...oyx/dot_general | solution.py:44
  108.3 4.9 %fusion.8 = bf16[8,64,6,1026]{3,1,2,0:T(8,128)(2,1)S(1)} fusion(bf16[8,64,1,1024]{3,1,2,0:T(8,128)(2,1)S(1)} %collective-permute-done.3, bf16[8,64,4,1024]{3,1,2,0:T(8,128)(2,1)S(1)} %copy-done.3, bf16[8,64,1,1024]{3,1,2,0:T(8,128)(2,1)S(1)} %collective-permute-done.2), kind=kLoop, calls=%fused_computation.19 | loop fusion | flops 37822464 | bytes 12595200 | tf_op jit(solution)/shard_map/concatenate | solution.py:16
  117.7 4.6 %fusion.22 = f32[8,4,1024,64]{2,3,1,0:T(8,128)} fusion(bf16[8,64,6,1026]{3,1,2,0:T(8,128)(2,1)S(1)} %fusion.8, bf16[9,64,64]{2,1,0:T(8,128)(2,1)S(1)} %copy-done.8), kind=kOutput, calls=%fused_computation.36 | convolution fusion | flops 268435456 | bytes 12599296 | tf_op jit(solution)/shard_map/oi,...iyx->...oyx/dot_general | solution.py:44
  126.8 4.6 %fusion.26 = f32[8,4,1024,64]{2,3,1,0:T(8,128)} fusion(bf16[8,64,6,1026]{3,1,2,0:T(8,128)(2,1)S(1)} %fusion.8, bf16[9,64,64]{2,1,0:T(8,128)(2,1)S(1)} %copy-done.8), kind=kOutput, calls=%fused_computation.40 | convolution fusion | flops 268435456 | bytes 12599296 | tf_op jit(solution)/shard_map/oi,...iyx->...oyx/dot_general | solution.py:44
  144.7 25.4 %multiply_reduce_fusion = (f32[8,4,1024]{2,1,0:T(4,128)S(1)}, f32[8,4,1024,64]{2,3,1,0:T(8,128)}) fusion(bf16[8,64,6,1026]{3,1,2,0:T(8,128)(2,1)S(1)} %fusion.8, bf16[9,64,64]{2,1,0:T(8,128)(2,1)S(1)} %copy-done.8, f32[8,4,1024,64]{2,3,1,0:T(8,128)} %fusion.18, f32[8,4,1024,64]{2,3,1,0:T(8,128)} %fusion.20, f32[8,4,1024,64]{2,3,1,0:T(8,128)} %fusion.22, ...), kind=kOutput, calls=%fused_computation.10 | convolution fusion | flops 289374208 | bytes 79839232 | tf_op jit(solution)/shard_map/oi,...iyx->...oyx/dot_general | solution.py:44
  170.1 6.8 %fusion.15 = bf16[8,64,4,1024]{3,1,2,0:T(8,128)(2,1)} fusion(f32[8,4,1024,64]{2,3,1,0:T(8,128)} %get-tuple-element.48, f32[8,4,1024]{2,1,0:T(4,128)S(1)} %add_rsqrt_fusion), kind=kLoop, calls=%fused_computation.28 | loop fusion | flops 6291456 | bytes 12713984 | tf_op jit(solution)/shard_map/convert_element_type | solution.py:52
  176.9 10.1 %copy.123 = bf16[8,64,4,1024]{1,0,3,2:T(8,128)(2,1)} copy(bf16[8,64,4,1024]{3,1,2,0:T(8,128)(2,1)} %fusion.15) | data formatting | bytes 8388608 | tf_op jit(solution)/shard_map/convert_element_type | solution.py:52
  187.0 7.7 %fusion.32 = (f32[8,2,512]{2,1,0:T(2,128)S(1)}, f32[8,2,512,128,1,1]{3,2,5,4,1,0:T(8,128)S(1)}) fusion(bf16[2,2,128,64,1,1]{2,3,1,0,5,4:T(8,128)(2,1)S(1)} %bitcast.397, bf16[8,64,2,2,512,2]{1,0,5,4,3,2:T(8,128)(2,1)} %bitcast.400), kind=kOutput, calls=%fused_computation.49 | convolution fusion | flops 538959872 | bytes 8486912 | tf_op jit(solution)/shard_map/abou,nuyaxb->noyx/dot_general | solution.py:63
  203.8 6.2 %collective-permute-done.4 = bf16[8,128,1,512]{1,3,2,0:T(8,128)(2,1)S(1)} collective-permute-done((bf16[8,128,1,512]{1,3,2,0:T(8,128)(2,1)S(1)}, bf16[8,128,1,512]{1,3,2,0:T(8,128)(2,1)S(1)}, u32[]{:S(2)}, u32[]{:S(2)}) %collective-permute-start.4) | collective-permute-done | bytes 1048608 | tf_op jit(solution)/shard_map/ppermute | solution.py:12
  234.9 11.8 %multiply_reduce_fusion.3 = (f32[8,2,512]{2,1,0:T(2,128)S(1)}, f32[8,2,512,128]{3,2,1,0:T(8,128)S(1)}) fusion(bf16[9,128,128]{2,1,0:T(8,128)(2,1)S(1)} %copy-done.6, bf16[8,128,4,514]{1,3,2,0:T(8,128)(2,1)S(1)} %fusion.13, f32[8,2,512,128]{3,2,1,0:T(8,128)} %fusion.42, f32[8,2,512,128]{3,2,1,0:T(8,128)} %fusion.52, f32[8,2,512,128]{3,2,1,0:T(8,128)} %fusion.54, ...), kind=kOutput, calls=%fused_computation.53 | convolution fusion | flops 278913024 | bytes 39911424 | tf_op jit(solution)/shard_map/oi,...iyx->...oyx/dot_general | solution.py:44
  264.9 5.4 %copy.145 = f32[8,128,2,512]{1,3,2,0:T(8,128)} copy(f32[8,128,2,512]{3,1,2,0:T(8,128)} %broadcast_bitcast_fusion) | data formatting | bytes 8388608 | tf_op jit(solution)/shard_map/mul | solution.py:159
  278.5 5.9 %broadcast_in_dim.52 = f32[8,16,2,2,512]{1,0,4,3,2:T(8,128)} broadcast(f32[8,16,2,512]{1,0,3,2:T(8,128)} %copy.151), dimensions={0,1,2,4} | broadcast | bytes 1572864 | tf_op jit(solution)/shard_map/broadcast_in_dim | solution.py:172
  284.5 10.4 %broadcast_in_dim.53 = f32[8,16,4,512,2]{1,0,4,3,2:T(8,128)} broadcast(f32[8,16,4,512]{1,0,3,2:T(8,128)} %bitcast.399), dimensions={0,1,2,3} | broadcast | bytes 3145728 | tf_op jit(solution)/shard_map/broadcast_in_dim | solution.py:172
  294.9 9.8 %copy.152 = f32[8,16,4,1024]{3,1,2,0:T(8,128)S(1)} copy(f32[8,16,4,1024]{1,0,3,2:T(8,128)} %bitcast.398) | data formatting | bytes 4194304 | tf_op jit(solution)/shard_map/mul | solution.py:176
  304.6 5.6 %mul.219 = f32[8,16,4,4,1024]{4,2,1,3,0:T(4,128)} broadcast(f32[8,16,4,1024]{3,1,2,0:T(8,128)S(1)} %copy.152), dimensions={0,1,3,4} | broadcast | bytes 10485760 | tf_op jit(solution)/shard_map/mul | solution.py:176
  310.3 10.0 %mul.220 = f32[8,64,4,1024]{3,1,2,0:T(8,128)} reshape(f32[8,16,4,4,1024]{4,2,1,3,0:T(4,128)} %mul.219) | data formatting | bytes 16777216 | tf_op jit(solution)/shard_map/mul | solution.py:176
  320.3 8.9 %multiply_reduce_fusion.2 = bf16[64,4,1024]{2,0,1:T(8,128)(2,1)} fusion(f32[8,64,4,1024]{3,1,2,0:T(8,128)} %mul.220, f32[8,4,1024,64]{2,3,1,0:T(8,128)} %get-tuple-element.48, f32[8,4,1024]{2,1,0:T(4,128)S(1)} %add_rsqrt_fusion), kind=kLoop, calls=%fused_computation.14 | loop fusion | flops 12320768 | bytes 17432576 | tf_op jit(solution)/shard_map/reduce_sum | solution.py:176
  332.4 27.1 %all-reduce.6.cloned.1.call-done = bf16[64,4,1024]{2,0,1:T(8,128)(2,1)} async-done(((bf16[64,4,1024]{2,0,1:T(8,128)(2,1)}), bf16[64,4,1024]{2,0,1:T(8,128)(2,1)}) %all-reduce.6.cloned.1.call-update) | async-done | bytes 524304 | tf_op jit(solution)/shard_map/psum | solution.py:179
  (125 shorter events, 138.2 us)
Async XLA Ops:
  6.5 180.4 %copy-start = (bf16[4,128,64]{1,2,0:T(8,128)(2,1)S(1)}, bf16[4,128,64]{1,2,0:T(8,128)(2,1)}, u32[]{:S(2)}) copy-start(bf16[4,128,64]{1,2,0:T(8,128)(2,1)} %param.19) | copy-start | bytes 196612
  6.5 322.8 %all-gather.4.cloned.1.call-start = ((), (), s32[]{:S(2)}) async-start(), calls=%async_computation | async-start | bytes 1572864 | tf_op jit(solution)/shard_map/all_gather | solution.py:21
  8.0 12.2 %collective-permute-start = (bf16[8,10,1,1024]{3,1,2,0:T(8,128)(2,1)S(1)}, bf16[8,10,1,1024]{3,1,2,0:T(8,128)(2,1)S(1)}, u32[]{:S(2)}, u32[]{:S(2)}) collective-permute-start(bf16[8,10,1,1024]{3,1,2,0:T(8,128)(2,1)S(1)} %get-tuple-element.39), channel_id=1, source_target_pairs={{0,1},{1,4},{4,5},{5,8},{8,9},{9,12},{12,13},{2,3},{3,6},{6,7},{7,... | collective-permute-start | bytes 491528 | tf_op jit(solution)/shard_map/ppermute | solution.py:12
  12.6 8.7 %copy-start.11 = (bf16[9,64,10]{1,2,0:T(8,128)(2,1)S(1)}, bf16[9,64,10]{1,2,0:T(8,128)(2,1)}, u32[]{:S(2)}) copy-start(bf16[9,64,10]{1,2,0:T(8,128)(2,1)} %param.17) | copy-start | bytes 34564
  12.6 7.7 %collective-permute-start.1 = (bf16[8,10,1,1024]{3,1,2,0:T(8,128)(2,1)S(1)}, bf16[8,10,1,1024]{3,1,2,0:T(8,128)(2,1)S(1)}, u32[]{:S(2)}, u32[]{:S(2)}) collective-permute-start(bf16[8,10,1,1024]{3,1,2,0:T(8,128)(2,1)S(1)} %get-tuple-element.40), channel_id=1, source_target_pairs={{1,0},{4,1},{5,4},{8,5},{9,8},{12,9},{13,12},{3,2},{6,3},{7,6},{10... | collective-permute-start | bytes 491528 | tf_op jit(solution)/shard_map/ppermute | solution.py:15
  21.3 18.7 %copy-start.5 = (bf16[8,10,6,1026]{3,1,2,0:T(8,128)(2,1)}, bf16[8,10,6,1026]{3,1,2,0:T(8,128)(2,1)S(1)}, u32[]{:S(2)}) copy-start(bf16[8,10,6,1026]{3,1,2,0:T(8,128)(2,1)S(1)} %fusion.69) | copy-start | bytes 2954884
  85.4 2.0 copy-start.2
  87.4 6.8 %copy-start.17 = (s32[8]{0:T(128)S(1)}, s32[8]{0:T(128)}, u32[]{:S(2)}) copy-start(s32[8]{0:T(128)} %param.16) | copy-start | bytes 100
  87.4 6.8 %copy-start.14 = (f32[16,4]{0,1:T(4,128)S(1)}, f32[16,4]{0,1:T(4,128)}, u32[]{:S(2)}) copy-start(f32[16,4]{0,1:T(4,128)} %param.22) | copy-start | bytes 772
  87.4 6.9 %copy-start.8 = (bf16[9,64,64]{2,1,0:T(8,128)(2,1)S(1)}, bf16[9,64,64]{2,1,0:T(8,128)(2,1)}, u32[]{:S(2)}) copy-start(bf16[9,64,64]{2,1,0:T(8,128)(2,1)} %param.18) | copy-start | bytes 221188
  88.6 15.6 %collective-permute-start.2 = (bf16[8,64,1,1024]{3,1,2,0:T(8,128)(2,1)}, bf16[8,64,1,1024]{3,1,2,0:T(8,128)(2,1)S(1)}, u32[]{:S(2)}, u32[]{:S(2)}) collective-permute-start(bf16[8,64,1,1024]{3,1,2,0:T(8,128)(2,1)} %get-tuple-element.30), channel_id=1, source_target_pairs={{0,1},{1,4},{4,5},{5,8},{8,9},{9,12},{12,13},{2,3},{3,6},{6,7},{7,... | collective-permute-start | bytes 3145736 | tf_op jit(solution)/shard_map/ppermute | solution.py:12
  92.2 16.1 %collective-permute-start.3 = (bf16[8,64,1,1024]{3,1,2,0:T(8,128)(2,1)S(1)}, bf16[8,64,1,1024]{3,1,2,0:T(8,128)(2,1)S(1)}, u32[]{:S(2)}, u32[]{:S(2)}) collective-permute-start(bf16[8,64,1,1024]{3,1,2,0:T(8,128)(2,1)S(1)} %get-tuple-element.32), channel_id=1, source_target_pairs={{1,0},{4,1},{5,4},{8,5},{9,8},{12,9},{13,12},{3,2},{6,3},{7,6},{10... | collective-permute-start | bytes 3145736 | tf_op jit(solution)/shard_map/ppermute | solution.py:15
  94.3 14.1 %copy-start.3 = (bf16[8,64,4,1024]{3,1,2,0:T(8,128)(2,1)S(1)}, bf16[8,64,4,1024]{3,1,2,0:T(8,128)(2,1)}, u32[]{:S(2)}) copy-start(bf16[8,64,4,1024]{3,1,2,0:T(8,128)(2,1)} %copy-done.2) | copy-start | bytes 12582916
  194.7 6.2 %copy-start.9 = (bf16[64,128]{1,0:T(8,128)(2,1)S(1)}, bf16[64,128]{1,0:T(8,128)(2,1)}, u32[]{:S(2)}) copy-start(bf16[64,128]{1,0:T(8,128)(2,1)} %param.21) | copy-start | bytes 49156
  194.7 6.3 %copy-start.12 = (s32[8,2,512]{2,1,0:T(2,128)S(1)}, s32[8,2,512]{2,1,0:T(2,128)}, u32[]{:S(2)}) copy-start(s32[8,2,512]{2,1,0:T(2,128)} %param.15) | copy-start | bytes 98308
  194.7 6.4 %copy-start.6 = (bf16[9,128,128]{2,1,0:T(8,128)(2,1)S(1)}, bf16[9,128,128]{2,1,0:T(8,128)(2,1)}, u32[]{:S(2)}) copy-start(bf16[9,128,128]{2,1,0:T(8,128)(2,1)} %param.20) | copy-start | bytes 884740
  196.4 13.7 %collective-permute-start.4 = (bf16[8,128,1,512]{1,3,2,0:T(8,128)(2,1)S(1)}, bf16[8,128,1,512]{1,3,2,0:T(8,128)(2,1)S(1)}, u32[]{:S(2)}, u32[]{:S(2)}) collective-permute-start(bf16[8,128,1,512]{1,3,2,0:T(8,128)(2,1)S(1)} %get-tuple-element.33), channel_id=1, source_target_pairs={{0,1},{1,4},{4,5},{5,8},{8,9},{9,12},{12,13},{2,3},{3,6},{6,7},{7,... | collective-permute-start | bytes 3145736 | tf_op jit(solution)/shard_map/ppermute | solution.py:12
  198.3 16.1 %collective-permute-start.5 = (bf16[8,128,1,512]{1,3,2,0:T(8,128)(2,1)S(1)}, bf16[8,128,1,512]{1,3,2,0:T(8,128)(2,1)S(1)}, u32[]{:S(2)}, u32[]{:S(2)}) collective-permute-start(bf16[8,128,1,512]{1,3,2,0:T(8,128)(2,1)S(1)} %get-tuple-element.34), channel_id=1, source_target_pairs={{1,0},{4,1},{5,4},{8,5},{9,8},{12,9},{13,12},{3,2},{6,3},{7,6},{10... | collective-permute-start | bytes 3145736 | tf_op jit(solution)/shard_map/ppermute | solution.py:15
  275.5 84.0 %all-reduce.6.cloned.1.call-start = ((), (), s32[]{:S(2)}) async-start(), calls=%async_computation.1 | async-start | bytes 1048576 | tf_op jit(solution)/shard_map/psum | solution.py:179
  320.3 10.3 %copy-start.16 = (bf16[128,128]{1,0:T(8,128)(2,1)S(1)}, bf16[128,128]{1,0:T(8,128)(2,1)}, u32[]{:S(2)}) copy-start(bf16[128,128]{1,0:T(8,128)(2,1)} %param.23) | copy-start | bytes 98308
  331.0 40.4 %copy-start.7 = (bf16[9,64,128]{2,1,0:T(8,128)(2,1)S(1)}, bf16[9,64,128]{2,1,0:T(8,128)(2,1)}, u32[]{:S(2)}) copy-start(bf16[9,64,128]{2,1,0:T(8,128)(2,1)} %param.25) | copy-start | bytes 442372
  360.5 7.7 %collective-permute-start.7 = (bf16[128,1,1024]{2,0,1:T(8,128)(2,1)S(1)}, bf16[128,1,1024]{2,0,1:T(8,128)(2,1)S(1)}, u32[]{:S(2)}, u32[]{:S(2)}) collective-permute-start(bf16[128,1,1024]{2,0,1:T(8,128)(2,1)S(1)} %get-tuple-element.35), channel_id=1, source_target_pairs={{1,0},{4,1},{5,4},{8,5},{9,8},{12,9},{13,12},{3,2},{6,3},{7,6},{10... | collective-permute-start | bytes 786440 | tf_op jit(solution)/shard_map/ppermute | solution.py:15
  363.1 6.3 %collective-permute-start.6 = (bf16[128,1,1024]{2,0,1:T(8,128)(2,1)S(1)}, bf16[128,1,1024]{2,0,1:T(8,128)(2,1)S(1)}, u32[]{:S(2)}, u32[]{:S(2)}) collective-permute-start(bf16[128,1,1024]{2,0,1:T(8,128)(2,1)S(1)} %get-tuple-element.36), channel_id=1, source_target_pairs={{0,1},{1,4},{4,5},{5,8},{8,9},{9,12},{12,13},{2,3},{3,6},{6,7},{7,... | collective-permute-start | bytes 786440 | tf_op jit(solution)/shard_map/ppermute | solution.py:12
  372.4 3.0 copy-start.1
  (4 other events, 7.2 us)
Sparse Core Ops, SparseCore 0:
  275.6 22.8 all-gather.3
  329.4 30.0 all-reduce.5
where the time goes:
time: 385 us; the launch traced here: 382 us
  matrix products  176 us (46%)
  local copies, waits for them, and re-layouts  75.4 us (20%)
  waiting for transfers between devices  48.2 us (13%)
  other arithmetic  39 us (10%)
  starting transfers between devices  22.2 us (6%)
  between operations  14.3 us (4%)
  blocking collectives  7.59 us (2%)
    dot_general x36, matrix products, conv_valid(): jnp.einsum('oi,...iyx->...oyx', weight[tap_index], window, preferred_elem...  164 us
    psum x1, waiting for transfers between devices, body(): skip_map = lax.psum(partial_value.astype(jnp.bfloat16), 'date')  27.1 us
    mul x3, local copies, waits for them, and re-layouts, body(): attn_fine[:, :, None] * fine_group  25.4 us
    broadcast_in_dim x2, local copies, waits for them, and re-layouts, body(): attn_fine = jnp.repeat(jnp.repeat(attention, 2, axis=2), 2, axis=3)  16.3 us
    ppermute x4, starting transfers between devices, extended_2(): lax.ppermute(lax.slice_in_dim(block, block.shape[dim] - width, None, axis...  13.3 us
    convert_element_type x2, other arithmetic, section(): return activate(conv_valid(extended, weight), 1).astype(jnp.bfloat16)  11.6 us
    ppermute x4, waiting for transfers between devices, extended_2(): lax.ppermute(lax.slice_in_dim(block, block.shape[dim] - width, None, axis...  10.6 us
    ppermute x4, waiting for transfers between devices, extended_2(): lax.ppermute(lax.slice_in_dim(block, 0, width, axis=dim), axis, backward)  10.4 us
  transfers between devices with their start and end apart: 10, of which 8 were waited for; matrix products, arithmetic and copies ran while one was open for 19% of the time, Pallas kernels for 0%

commit v1 on v0

v1 whole, which is shorter than its diff:
```python
import functools

import jax
import jax.numpy as jnp
import numpy as np
from jax import lax
from jax.experimental import pallas as pl
from jax.experimental.pallas import tpu as pltpu
from jax.sharding import PartitionSpec as P

BF = jnp.bfloat16
F32 = jnp.float32
NEG = -1e30
ROWS = ("tile", "row")


def dot(a, b):
    return lax.dot_general(a, b, (((1,), (0,)), ((), ())), preferred_element_type=F32)


def act(y):
    ms = jnp.mean(y * y, axis=1, keepdims=True)
    return jnp.maximum(y * lax.rsqrt(ms + 1e-5), 0.0)


def from_left(x):
    lane = lax.broadcasted_iota(jnp.int32, x.shape, x.ndim - 1)
    return jnp.where(lane == 0, 0.0, pltpu.roll(x, 1, x.ndim - 1))


def from_right(x):
    n = x.shape[-1]
    lane = lax.broadcasted_iota(jnp.int32, x.shape, x.ndim - 1)
    return jnp.where(lane == n - 1, 0.0, pltpu.roll(x, n - 1, x.ndim - 1))


COL = ((1, 2, 0, None), (0, 1, None, 2))


def paired(w, order):
    lines = []
    for ro in range(2):
        for po in range(2):
            line = []
            for ri in range(4):
                a = ri - ro
                for v, lo, hi in order:
                    b = COL[po][v]
                    if b is None or not 0 <= a < 3:
                        line.append(jnp.zeros((w.shape[1], hi - lo), w.dtype))
                    else:
                        line.append(w[3 * a + b, :, lo:hi])
            lines.append(jnp.concatenate(line, axis=1))
    return jnp.concatenate(lines, axis=0)


def coarse_weight(w):
    lines = []
    for ro in range(2):
        line = []
        for ri in range(4):
            a = ri - ro
            for b in (1, 0, 2):
                if 0 <= a < 3:
                    line.append(w[3 * a + b])
                else:
                    line.append(jnp.zeros(w.shape[1:], w.dtype))
        lines.append(jnp.concatenate(line, axis=1))
    return jnp.concatenate(lines, axis=0)


def regroup(w, axis, heads):
    axis = axis % w.ndim
    n = w.shape[axis] // heads
    shape = w.shape[:axis] + (heads, n) + w.shape[axis + 1:]
    return jnp.swapaxes(w.reshape(shape), axis, axis + 1).reshape(w.shape)


def encode_kernel(heads, fine_ch, coarse_ch, edge_ref, img_ref, cloud_ref, sel_ref, w1_ref, w2_ref, wd_ref, wc_ref,
                  kw_ref, kb_ref, q_ref, ml_ref, out_ref, xi, s1, s2, m_s, l_s, a_s, k_s):
    t = pl.program_id(0)
    half = xi.shape[1]
    bands = 16
    top, bottom = edge_ref[0], edge_ref[1]

    @pl.when(t == 0)
    def _():
        m_s[...] = jnp.full(m_s.shape, NEG, F32)
        l_s[...] = jnp.zeros(l_s.shape, F32)
        a_s[...] = jnp.zeros(a_s.shape, F32)
        k_s[...] = jnp.zeros(k_s.shape, F32)

    sel = sel_ref[...]
    es, os = [], []
    for q in range(2 * half // 256):
        y = dot(img_ref[0, :, 256 * q:256 * q + 256], sel)
        es.append(y[:, :128])
        os.append(y[:, 128:])
    e = jnp.concatenate(es, axis=1)
    o = jnp.concatenate(os, axis=1)
    variants = (e, o, from_left(o), from_right(e))
    for v, x in enumerate(variants):
        x = x.astype(BF)
        for r in range(12):
            xi[64 * r + bands * v:64 * r + bands * v + bands, :] = x[bands * r:bands * r + bands]
    for g in range(5):
        y = dot(w1_ref[...], xi[128 * g:128 * g + 256, :])
        y = act(y.reshape(4, fine_ch, half))
        for ro in range(2):
            k = 2 * g + ro
            e, o = y[2 * ro], y[2 * ro + 1]
            if k < 3:
                e, o = e * top, o * top
            if k > 6:
                e, o = e * bottom, o * bottom
            base = 4 * fine_ch * k
            for v, x in enumerate((e, o, from_left(o), from_right(e))):
                s1[base + fine_ch * v:base + fine_ch * (v + 1), :] = x.astype(BF)
    fines = []
    for g in range(4):
        y = dot(w2_ref[...], s1[8 * fine_ch * g:8 * fine_ch * g + 16 * fine_ch, :])
        f = act(y.reshape(4, fine_ch, half)).reshape(4 * fine_ch, half).astype(BF)
        if g in (1, 2):
            fines.append(f)
        low = act(dot(wd_ref[...], f)[None])[0]
        if g == 0:
            low = low * top
        if g == 3:
            low = low * bottom
        base = 3 * coarse_ch * g
        for v, x in enumerate((low, from_left(low), from_right(low))):
            s2[base + coarse_ch * v:base + coarse_ch * (v + 1), :] = x.astype(BF)
    y = dot(wc_ref[...], s2[...])
    coarse = act(y.reshape(2, coarse_ch, half)).reshape(2 * coarse_ch, half).astype(BF)
    km = (dot(kw_ref[...], coarse) + kb_ref[0]) * q_ref[...]
    km = km.reshape(2, km.shape[0] // (2 * heads), heads, half)
    scores = 0.5 * jnp.sum(km, axis=1)
    for rr in range(2):
        valid = cloud_ref[0, rr:rr + 1, :] == 1
        s = jnp.where(valid, scores[rr], NEG)
        m_old = m_s[rr]
        m_new = jnp.maximum(m_old, s)
        f = jnp.exp(m_old - m_new)
        p = jnp.where(valid, jnp.exp(s - m_new), 0.0)
        m_s[rr] = m_new
        l_s[rr] = l_s[rr] * f + p
        c = coarse[coarse_ch * rr:coarse_ch * (rr + 1)].reshape(-1, heads, half).astype(F32)
        a_s[rr] = a_s[rr] * f[None] + p[None] * c
        c = fines[rr].reshape(-1, heads, half).astype(F32)
        k_s[rr] = k_s[rr] * f[None] + p[None] * c

    @pl.when(t == pl.num_programs(0) - 1)
    def _():
        for rr in range(2):
            total = l_s[rr]
            ml_ref[heads * rr:heads * (rr + 1), :] = m_s[rr]
            ml_ref[heads * (2 + rr):heads * (3 + rr), :] = total
            inv = (1.0 / jnp.maximum(total, 0.5))[None]
            a = (a_s[rr] * inv).reshape(coarse_ch, half)
            out_ref[coarse_ch * rr:coarse_ch * (rr + 1), :] = a.astype(BF)
            base = 2 * coarse_ch + 4 * fine_ch * rr
            k = (k_s[rr] * inv).reshape(4 * fine_ch, half)
            out_ref[base:base + 4 * fine_ch, :] = k.astype(BF)


def combine_kernel(heads, fine_ch, coarse_ch, ml_ref, ab_ref, wo_ref, wu_ref, out_ref):
    dates = ml_ref.shape[0]
    width = ml_ref.shape[2]
    for rr in range(2):
        ms = [ml_ref[d, heads * rr:heads * (rr + 1), :] for d in range(dates)]
        top = functools.reduce(jnp.maximum, ms)
        ws = [ml_ref[d, heads * (2 + rr):heads * (3 + rr), :] * jnp.exp(ms[d] - top) for d in range(dates)]
        inv = 1.0 / functools.reduce(jnp.add, ws)
        ws = [(w * inv)[None] for w in ws]

        def mix(base, size):
            parts = [
                ws[d] * ab_ref[d, base:base + size, :].reshape(-1, heads, width).astype(F32) for d in range(dates)
            ]
            return functools.reduce(jnp.add, parts).reshape(size, width).astype(BF)

        agg = mix(coarse_ch * rr, coarse_ch)
        skip = mix(2 * coarse_ch + 4 * fine_ch * rr, 4 * fine_ch)
        co = act(dot(wo_ref[...], agg)[None])[0].astype(BF)
        up = dot(wu_ref[...], co).astype(BF)
        n = 2 * fine_ch
        for a in range(2):
            base = 2 * n * (2 * rr + a)
            out_ref[base:base + n, :] = up[n * a:n * (a + 1)]
            out_ref[base + n:base + 2 * n, :] = skip[n * a:n * (a + 1)]


def decode_kernel(fine_ch, off_ref, top_ref, mid_ref, low_ref, wdec_ref, cls_ref, bias_ref, out_ref, s3):
    width = s3.shape[1]
    n = 4 * fine_ch
    rows = mid_ref.shape[0] // n
    for k in range(rows + 2):
        if k == 0:
            x = top_ref[...]
        elif k == rows + 1:
            x = low_ref[...]
        else:
            x = mid_ref[n * (k - 1):n * k, :]
        base = 2 * n * k
        s3[base:base + n, :] = x
        x = x.astype(F32).reshape(2, 2, fine_ch, width)
        half = 2 * fine_ch
        s3[base + n:base + n + half, :] = from_left(x[:, 1].reshape(half, width)).astype(BF)
        s3[base + n + half:base + 2 * n, :] = from_right(x[:, 0].reshape(half, width)).astype(BF)
    share = out_ref.shape[2]
    src = lax.broadcasted_iota(jnp.int32, (2 * width, share), 0)
    dst = lax.broadcasted_iota(jnp.int32, (2 * width, share), 1)
    pick = (src == off_ref[0] + lax.shift_right_logical(dst, 1) + (dst & 1) * width).astype(F32).astype(BF)
    for g in range(rows // 2):
        y = dot(wdec_ref[...], s3[4 * n * g:4 * n * g + 8 * n, :])
        y = act(y.reshape(4, fine_ch, width)).astype(BF)
        for ro in range(2):
            d = jnp.concatenate([y[2 * ro], y[2 * ro + 1]], axis=1)
            d = dot(d, pick).astype(BF)
            out_ref[:, 2 * g + ro, :] = dot(cls_ref[...], d) + bias_ref[...]


VMEM = pl.BlockSpec(memory_space=pltpu.VMEM)
SMEM = pl.BlockSpec(memory_space=pltpu.SMEM)


def neighbour_shift(x, step):
    count = lax.axis_size(ROWS)
    if step > 0:
        pairs = [(i, i + 1) for i in range(count - 1)]
    else:
        pairs = [(i + 1, i) for i in range(count - 1)]
    return lax.ppermute(x, ROWS, pairs)


def body(images, clouds, day_of_year, conv_first, conv_second, conv_down, conv_coarse, key_weight, query_weight,
         out_weight, up_weight, dec_weight, cls_weight, cls_bias):
    dates, bands, rows, cols = images.shape
    half = cols // 2
    fine_ch = conv_second.shape[1]
    coarse_ch = conv_coarse.shape[1]
    heads, key_size = query_weight.shape
    classes = cls_weight.shape[0]
    groups = lax.axis_size("date")
    me = lax.axis_index("date")
    band = lax.axis_index(ROWS)
    count = lax.axis_size(ROWS)

    above = neighbour_shift(images, 1)
    below = neighbour_shift(images, -1)
    ext = jnp.concatenate([above, images, below], axis=2)
    ext = jnp.pad(jnp.transpose(ext, (0, 2, 1, 3)), ((0, 0), (0, 0), (0, 16 - bands), (0, 0)))
    ext = ext.reshape(dates, 12 * 16, cols)

    edges = jnp.stack([(band > 0).astype(F32), (band < count - 1).astype(F32)])

    sel = np.zeros((256, 256), np.float32)
    for i in range(128):
        sel[2 * i, i] = 1
        sel[2 * i + 1, 128 + i] = 1
    sel = jnp.asarray(sel, BF)

    w1 = paired(jnp.pad(conv_first, ((0, 0), (0, 0), (0, 16 - bands))), [(v, 0, 16) for v in range(4)])
    w2 = paired(regroup(conv_second, 1, heads), [(v, 0, fine_ch) for v in range(4)])
    wd = jnp.transpose(regroup(conv_down, 2, heads), (1, 0, 2)).reshape(coarse_ch, 4 * fine_ch)
    wc = coarse_weight(regroup(conv_coarse, 1, heads))
    kw = regroup(regroup(key_weight, 0, heads), 1, heads)
    zero = jnp.zeros_like(kw)
    kw2 = jnp.concatenate([jnp.concatenate([kw, zero], 1), jnp.concatenate([zero, kw], 1)], 0)
    half_ch = coarse_ch // 2
    freqs = jnp.power(1000.0, -2.0 * jnp.arange(half_ch, dtype=F32) / coarse_ch)
    angles = day_of_year.astype(F32)[:, None] * freqs[None, :]
    encoding = jnp.concatenate([jnp.sin(angles), jnp.cos(angles)], axis=1)
    kb = jnp.dot(encoding, key_weight.astype(F32).T, precision=lax.Precision.HIGHEST)
    kb = regroup(kb, 1, heads)
    kb = jnp.concatenate([kb, kb], axis=1)[:, :, None]
    qv = jnp.transpose(query_weight).reshape(-1)
    qv = jnp.concatenate([qv, qv])[:, None]

    nk = 2 * heads * key_size
    total = 2 * coarse_ch + 8 * fine_ch
    const = lambda *shape: pl.BlockSpec(shape, lambda t: (0,) * len(shape))
    ml, ab = pl.pallas_call(
        functools.partial(encode_kernel, heads, fine_ch, coarse_ch),
        grid=(dates,),
        in_specs=[
            SMEM,
            pl.BlockSpec((1, 192, cols), lambda t: (t, 0, 0)),
            pl.BlockSpec((1, 2, half), lambda t: (t, 0, 0)),
            const(256, 256),
            const(*w1.shape),
            const(*w2.shape),
            const(*wd.shape),
            const(*wc.shape),
            const(*kw2.shape),
            pl.BlockSpec((1, nk, 1), lambda t: (t, 0, 0)),
            const(nk, 1),
        ],
        out_specs=[const(4 * heads, half), const(total, half)],
        out_shape=[jax.ShapeDtypeStruct((4 * heads, half), F32), jax.ShapeDtypeStruct((total, half), BF)],
        scratch_shapes=[
            pltpu.VMEM((12 * 64, half), BF),
            pltpu.VMEM((40 * fine_ch, half), BF),
            pltpu.VMEM((12 * coarse_ch, half), BF),
            pltpu.VMEM((2, heads, half), F32),
            pltpu.VMEM((2, heads, half), F32),
            pltpu.VMEM((2, coarse_ch // heads, heads, half), F32),
            pltpu.VMEM((2, 4 * fine_ch // heads, heads, half), F32),
        ],
        compiler_params=pltpu.CompilerParams(vmem_limit_bytes=48 * 1024 * 1024),
    )(edges, ext, clouds, sel, w1, w2, wd, wc, kw2, kb, qv)

    per = half // groups
    spans = []
    for k in range(groups):
        lo = max(0, (k * per - 1) // 128)
        hi = min(half // 128 - 1, (k * per + per) // 128)
        spans.append((lo, hi))
    width = max(hi - lo + 1 for lo, hi in spans) * 128
    starts = jnp.asarray([min(lo * 128, half - width) for lo, hi in spans], jnp.int32)

    def window(x, k):
        return lax.dynamic_slice_in_dim(x, starts[k], width, 1)

    mls, abs_ = [window(ml, me)], [window(ab, me)]
    for step in range(1, groups):
        to = lax.rem(me + step, groups)
        pairs = [(i, (i + step) % groups) for i in range(groups)]
        mls.append(lax.ppermute(window(ml, to), "date", pairs))
        abs_.append(lax.ppermute(window(ab, to), "date", pairs))
    joined = pl.pallas_call(
        functools.partial(combine_kernel, heads, fine_ch, coarse_ch),
        in_specs=[VMEM] * 4,
        out_specs=VMEM,
        out_shape=jax.ShapeDtypeStruct((rows * 4 * fine_ch, width), BF),
        compiler_params=pltpu.CompilerParams(vmem_limit_bytes=48 * 1024 * 1024),
    )(jnp.stack(mls), jnp.stack(abs_), regroup(out_weight, 1, heads), up_weight.reshape(4 * fine_ch, coarse_ch))

    n = 4 * fine_ch
    top = neighbour_shift(joined[-n:], 1)
    low = neighbour_shift(joined[:n], -1)
    dec = jnp.concatenate([dec_weight[:, :, :fine_ch], regroup(dec_weight[:, :, fine_ch:], 2, heads)], axis=2)
    up_part, skip_part = (0, fine_ch), (fine_ch, 2 * fine_ch)
    wdec = paired(dec, [(0, *up_part), (1, *up_part), (0, *skip_part), (1, *skip_part),
                        (2, *up_part), (2, *skip_part), (3, *up_part), (3, *skip_part)])
    offset = (me * per - starts[me]).astype(jnp.int32).reshape(1)
    return pl.pallas_call(
        functools.partial(decode_kernel, fine_ch),
        in_specs=[SMEM] + [VMEM] * 6,
        out_specs=VMEM,
        out_shape=jax.ShapeDtypeStruct((classes, rows, cols // groups), F32),
        scratch_shapes=[pltpu.VMEM(((rows + 2) * 2 * n, width), BF)],
        compiler_params=pltpu.CompilerParams(vmem_limit_bytes=48 * 1024 * 1024),
    )(offset, top, joined, low, wdec, cls_weight, cls_bias[:, None])


def solution(mesh):
    return jax.shard_map(
        body,
        mesh=mesh,
        in_specs=(
            P("date", None, ("grp", "tile", "row"), None),
            P("date", ("grp", "tile", "row"), None),
            P(("grp", "date")),
        ) + (P(),) * 11,
        out_specs=P(None, ("grp", "tile", "row"), "date"),
        check_vma=False,
    )
```

time: 385 us -> 98.3 us (0.26)
  matrix products: 176 us -> 0.21 us
  local copies, waits for them, and re-layouts: 75.4 us -> 22.1 us
  Pallas kernels: 0 us -> 39.4 us
  other arithmetic: 39 us -> 4.88 us
  waiting for transfers between devices: 48.2 us -> 16.3 us
  between operations: 14.3 us -> 0.64 us
  starting transfers between devices: 22.2 us -> 14.2 us
  blocking collectives: 7.59 us -> 0 us
    dot_general x42 -> x1, matrix products: 176 us -> 0.21 us  [body(): jnp.dot(encoding, key_weight.astype(F32).T, precision=lax.Precision.HIGHEST)]
    pallas_call x0 -> x3, Pallas kernels: none -> 39.4 us  [the longest x1 35.4 us: body(): pl.pallas_call(functools.partial(encode_kernel, heads, fine_ch, coarse_ch...]
    mul x5 -> x0, local copies, waits for them, and re-layouts: 33.2 us -> none  [the longest x3 25.4 us: body(): attn_fine[:, :, None] * fine_group]
    psum x1 -> x0, waiting for transfers between devices: 27.1 us -> none  [body(): skip_map = lax.psum(partial_value.astype(jnp.bfloat16), 'date')]
    broadcast_in_dim x2 -> x3, local copies, waits for them, and re-layouts: 16.3 us -> 1.1 us  [the longest x1 0.76 us: body(): cls_bias[:, None]]
    reduce_sum x4 -> x0, other arithmetic: 14.6 us -> none  [the longest x1 8.95 us: body(): jnp.sum(attn_fine[:, :, None] * fine_group, axis=0)]
    convert_element_type x4 -> x1, other arithmetic: 13 us -> 0.01 us  [body(): angles = day_of_year.astype(F32)[:, None] * freqs[None, :]]
    convert_element_type x3 -> x0, local copies, waits for them, and re-layouts: 11.2 us -> none  [the longest x1 10.1 us: section(): return activate(conv_valid(extended, weight), 1).astype(jnp.bfloat16)]
  transfers between devices with their start and end apart: 10 -> 6, of which waited for: 8 -> 3; matrix products, arithmetic and copies ran while one was open for 19% -> 22% of each run, Pallas kernels for 0% -> 0%
where the time goes in v1:
time: 98.3 us; the launch traced here: 97.8 us
  Pallas kernels  39.4 us (40%)
  local copies, waits for them, and re-layouts  22.1 us (22%)
  waiting for transfers between devices  16.3 us (17%)
  starting transfers between devices  14.2 us (14%)
  other arithmetic  4.88 us (5%)
    pallas_call x1, Pallas kernels, body(): pl.pallas_call(functools.partial(encode_kernel, heads, fine_ch, coarse_ch...  35.4 us
    ppermute x4, starting transfers between devices, neighbour_shift(): return lax.ppermute(x, ROWS, pairs)  12.6 us
    ppermute x1, waiting for transfers between devices, body(): mls.append(lax.ppermute(window(ml, to), 'date', pairs))  11.4 us
    unnamed x38, local copies, waits for them, and re-layouts  9.67 us
    ppermute x4, waiting for transfers between devices, neighbour_shift(): return lax.ppermute(x, ROWS, pairs)  4.97 us
    concatenate x12, local copies, waits for them, and re-layouts, paired(): lines.append(jnp.concatenate(line, axis=1))  4.1 us
    pallas_call x1, Pallas kernels, body(): pl.pallas_call(functools.partial(decode_kernel, fine_ch), in_specs=[SMEM]...  3.25 us
    pad x1, local copies, waits for them, and re-layouts, body(): jnp.pad(jnp.transpose(ext, (0, 2, 1, 3)), ((0, 0), (0, 0), (0, 16 - bands...  2.43 us
  transfers between devices with their start and end apart: 6, of which 3 were waited for; matrix products, arithmetic and copies ran while one was open for 22% of the time, Pallas kernels for 0%

profile of v1, /device:TPU:1, one launch (start us, length us, event | category | flops | bytes accessed | tf_op | source)
XLA Modules:
  0.0 97.8 jit_solution(3683189988960768774)
XLA Ops:
  0.0 2.1 %collective-permute-start.1 = (bf16[8,10,4,1024]{3,2,1,0:T(4,128)(2,1)}, bf16[8,10,4,1024]{3,2,1,0:T(4,128)(2,1)S(1)}, u32[]{:S(2)}, u32[]{:S(2)}) collective-permute-start(bf16[8,10,4,1024]{3,2,1,0:T(4,128)(2,1)} %param.16), channel_id=1, source_target_pairs={{1,0},{4,1},{5,4},{8,5},{9,8},{12,9},{13,12},{3,2},{6,3},{7,6},{10... | collective-permute-start | bytes 1966088 | tf_op jit(solution)/shard_map/ppermute | solution.py:233
  2.1 4.6 %collective-permute-start = (bf16[8,10,4,1024]{3,2,1,0:T(4,128)(2,1)}, bf16[8,10,4,1024]{3,2,1,0:T(4,128)(2,1)S(1)}, u32[]{:S(2)}, u32[]{:S(2)}) collective-permute-start(bf16[8,10,4,1024]{3,2,1,0:T(4,128)(2,1)} %param.16), channel_id=1, source_target_pairs={{0,1},{1,4},{4,5},{5,8},{8,9},{9,12},{12,13},{2,3},{3,6},{6,7},{7,... | collective-permute-start | bytes 1966088 | tf_op jit(solution)/shard_map/ppermute | solution.py:233
  6.7 0.9 copy.90
  7.7 0.9 copy.159
  8.6 1.0 %copy.158 = bf16[9,16,8,128]{3,1,2,0:T(8,128)(2,1)S(1)} copy(bf16[9,16,8,128]{3,2,1,0:T(8,128)(2,1)} %bitcast.158) | data formatting | bytes 589824 | tf_op jit(solution)/shard_map/reshape | solution.py:76
  18.4 0.7 concatenate.77
  19.1 0.7 concatenate.76
  20.2 0.8 concatenate.81
  22.2 0.8 pad_maximum_fusion.5.w1_ref
  23.0 0.9 pad_maximum_fusion.3.w2_ref
  23.9 1.2 %pad_maximum_fusion.2.wc_ref = bf16[256,1536]{1,0:T(8,128)(2,1)S(1)} fusion(bf16[128,1536]{1,0:T(8,128)(2,1)} %copy-done.6, bf16[128,1536]{1,0:T(8,128)(2,1)} %constant_dynamic-update-slice_fusion), kind=kLoop, calls=%fused_computation.3 | loop fusion | flops 1572864 | bytes 1572864 | tf_op jit(solution)/shard_map/concatenate | solution.py:69
  25.1 1.4 %maximum_bitcast_fusion = bf16[8,12,10,1024]{3,1,2,0:T(8,128)(2,1)S(1)} fusion(bf16[8,10,4,1024]{3,2,1,0:T(4,128)(2,1)S(1)} %collective-permute-done.1, bf16[8,10,4,1024]{3,2,1,0:T(4,128)(2,1)S(1)} %copy-done.4, bf16[8,10,4,1024]{3,2,1,0:T(4,128)(2,1)S(1)} %collective-permute-done), kind=kLoop, calls=%fused_computation | loop fusion | flops 5898240 | bytes 3932160 | tf_op jit(solution)/shard_map/transpose | solution.py:252
  26.5 1.4 %copy.155 = bf16[8,12,10,1024]{3,2,1,0:T(8,128)(2,1)S(1)} copy(bf16[8,12,10,1024]{3,1,2,0:T(8,128)(2,1)S(1)} %maximum_bitcast_fusion) | data formatting | bytes 3932160
  28.0 2.4 %pad.10.clone = bf16[8,12,16,1024]{3,2,1,0:T(8,128)(2,1)} pad(bf16[8,12,10,1024]{3,2,1,0:T(8,128)(2,1)S(1)} %copy.155, bf16[]{:T(256)} %constant.13.clone.1), padding=0_0x0_0x0_6x0_0 | pad | bytes 5111810 | tf_op jit(solution)/shard_map/jit(_pad)/pad | solution.py:252
  30.4 35.4 %shard_map.154 = (f32[64,512]{1,0:T(8,128)S(1)}, bf16[768,512]{1,0:T(8,128)(2,1)S(1)}) custom-call(f32[2]{0:T(128)S(1)} %add_convert_fusion.edge_ref, bf16[8,192,1024]{2,1,0:T(8,128)(2,1)} %bitcast.116, s32[8,2,512]{2,1,0:T(2,128)S(1)} %copy-done.2, bf16[256,256]{1,0:T(8,128)(2,1)S(1)} %copy-done, bf16[256,256]{1,0:T(8,128)(2,1)S(1)} %pad_maximum_fusion.5.w1_ref, ...), custom_call_target="tpu_custom_call" | custom-call | tf_op jit(solution)/shard_map/pallas_call | solution.py:283
  65.9 1.3 %collective-permute-start.3 = (bf16[768,384]{1,0:T(8,128)(2,1)S(1)}, bf16[768,384]{1,0:T(8,128)(2,1)S(1)}, u32[]{:S(2)}, u32[]{:S(2)}) collective-permute-start(bf16[768,384]{1,0:T(8,128)(2,1)S(1)} %get-tuple-element.12), channel_id=1, source_target_pairs={{0,2},{2,0},{1,3},{3,1},{4,6},{6,4},{5,7},{7,5},{8,10},{10,8},{9,1... | collective-permute-start | bytes 1769480 | tf_op jit(solution)/shard_map/ppermute | solution.py:330
  69.3 0.9 copy.103
  70.3 0.8 copy.152.bias_ref
  71.0 11.4 %collective-permute-done.2 = f32[64,384]{1,0:T(8,128)S(1)} collective-permute-done((f32[64,384]{1,0:T(8,128)S(1)}, f32[64,384]{1,0:T(8,128)S(1)}, u32[]{:S(2)}, u32[]{:S(2)}) %collective-permute-start.2) | collective-permute-done | bytes 98336 | tf_op jit(solution)/shard_map/ppermute | solution.py:329
  82.6 0.8 shard_map.155.mid_ref
  83.5 4.0 %collective-permute-start.4 = (bf16[256,384]{1,0:T(8,128)(2,1)S(1)}, bf16[256,384]{1,0:T(8,128)(2,1)S(1)}, u32[]{:S(2)}, u32[]{:S(2)}) collective-permute-start(bf16[256,384]{1,0:T(8,128)(2,1)S(1)} %get-tuple-element.10), channel_id=1, source_target_pairs={{0,1},{1,4},{4,5},{5,8},{8,9},{9,12},{12,13},{2,3},{3,6},{6,7},{7,... | collective-permute-start | bytes 589832 | tf_op jit(solution)/shard_map/ppermute | solution.py:233
  87.5 1.9 %collective-permute-start.5 = (bf16[256,384]{1,0:T(8,128)(2,1)S(1)}, bf16[256,384]{1,0:T(8,128)(2,1)S(1)}, u32[]{:S(2)}, u32[]{:S(2)}) collective-permute-start(bf16[256,384]{1,0:T(8,128)(2,1)S(1)} %get-tuple-element.9), channel_id=1, source_target_pairs={{1,0},{4,1},{5,4},{8,5},{9,8},{12,9},{13,12},{3,2},{6,3},{7,6},{10... | collective-permute-start | bytes 589832 | tf_op jit(solution)/shard_map/ppermute | solution.py:233
  90.1 4.4 %collective-permute-done.5.low_ref = bf16[256,384]{1,0:T(8,128)(2,1)S(1)} collective-permute-done((bf16[256,384]{1,0:T(8,128)(2,1)S(1)}, bf16[256,384]{1,0:T(8,128)(2,1)S(1)}, u32[]{:S(2)}, u32[]{:S(2)}) %collective-permute-start.5) | collective-permute-done | bytes 196640 | tf_op jit(solution)/shard_map/ppermute | solution.py:233
  94.5 3.3 %shard_map.156 = f32[20,4,512]{2,1,0:T(4,128)} custom-call(s32[1]{0:T(128)} %bitcast.off_ref, bf16[256,384]{1,0:T(8,128)(2,1)S(1)} %collective-permute-done.4.top_ref, bf16[1024,384]{1,0:T(8,128)(2,1)S(1)} %shard_map.155.mid_ref, bf16[256,384]{1,0:T(8,128)(2,1)S(1)} %collective-permute-done.5.low_ref, bf16[256,2048]{1,0:T(8,128)(2,1)S(1)} %pad_maximum_fusion.1.wdec_ref, ...), custom_call_target="tpu_custom_call" | custom-call | tf_op jit(solution)/shard_map/pallas_call | solution.py:347
  (106 shorter events, 13.2 us)
Async XLA Ops:
  0.0 16.6 %copy-start.10 = (s32[8]{0:T(128)S(1)}, s32[8]{0:T(128)}, u32[]{:S(2)}) copy-start(s32[8]{0:T(128)} %param.18) | copy-start | bytes 100
  0.0 16.7 %copy-start.7 = (bf16[64,128]{1,0:T(8,128)(2,1)S(1)}, bf16[64,128]{1,0:T(8,128)(2,1)}, u32[]{:S(2)}) copy-start(bf16[64,128]{1,0:T(8,128)(2,1)} %param.23) | copy-start | bytes 49156
  0.0 17.2 %copy-start.9 = (f32[16,4]{0,1:T(4,128)S(1)}, f32[16,4]{0,1:T(4,128)}, u32[]{:S(2)}) copy-start(f32[16,4]{0,1:T(4,128)} %param.24) | copy-start | bytes 772
  0.0 25.1 %collective-permute-start.1 = (bf16[8,10,4,1024]{3,2,1,0:T(4,128)(2,1)}, bf16[8,10,4,1024]{3,2,1,0:T(4,128)(2,1)S(1)}, u32[]{:S(2)}, u32[]{:S(2)}) collective-permute-start(bf16[8,10,4,1024]{3,2,1,0:T(4,128)(2,1)} %param.16), channel_id=1, source_target_pairs={{1,0},{4,1},{5,4},{8,5},{9,8},{12,9},{13,12},{3,2},{6,3},{7,6},{10... | collective-permute-start | bytes 1966088 | tf_op jit(solution)/shard_map/ppermute | solution.py:233
  2.1 23.0 %collective-permute-start = (bf16[8,10,4,1024]{3,2,1,0:T(4,128)(2,1)}, bf16[8,10,4,1024]{3,2,1,0:T(4,128)(2,1)S(1)}, u32[]{:S(2)}, u32[]{:S(2)}) collective-permute-start(bf16[8,10,4,1024]{3,2,1,0:T(4,128)(2,1)} %param.16), channel_id=1, source_target_pairs={{0,1},{1,4},{4,5},{5,8},{8,9},{9,12},{12,13},{2,3},{3,6},{6,7},{7,... | collective-permute-start | bytes 1966088 | tf_op jit(solution)/shard_map/ppermute | solution.py:233
  9.7 11.4 %copy-start.8 = (bf16[4,128,64]{1,2,0:T(8,128)(2,1)S(1)}, bf16[4,128,64]{1,2,0:T(8,128)(2,1)}, u32[]{:S(2)}) copy-start(bf16[4,128,64]{1,2,0:T(8,128)(2,1)} %param.21) | copy-start | bytes 196612
  15.4 2.0 %copy-start.6 = (bf16[128,1536]{1,0:T(8,128)(2,1)}, bf16[128,1536]{1,0:T(8,128)(2,1)S(1)}, u32[]{:S(2)}) copy-start(bf16[128,1536]{1,0:T(8,128)(2,1)S(1)} %get-tuple-element.61) | copy-start | bytes 1179652
  15.4 6.5 %copy-start.5 = (bf16[9,64,128]{2,1,0:T(8,128)(2,1)S(1)}, bf16[9,64,128]{2,1,0:T(8,128)(2,1)}, u32[]{:S(2)}) copy-start(bf16[9,64,128]{2,1,0:T(8,128)(2,1)} %param.27) | copy-start | bytes 442372
  21.4 3.7 %copy-start.4 = (bf16[8,10,4,1024]{3,2,1,0:T(4,128)(2,1)S(1)}, bf16[8,10,4,1024]{3,2,1,0:T(4,128)(2,1)}, u32[]{:S(2)}) copy-start(bf16[8,10,4,1024]{3,2,1,0:T(4,128)(2,1)} %param.16) | copy-start | bytes 1966084
  27.9 2.5 %copy-start = (bf16[256,256]{1,0:T(8,128)(2,1)S(1)}, bf16[256,256]{1,0:T(8,128)(2,1)}, u32[]{:S(2)}) copy-start(bf16[256,256]{1,0:T(8,128)(2,1)} %constant.46.clone.sel_ref) | copy-start | bytes 393220
  28.0 2.5 %copy-start.2 = (s32[8,2,512]{2,1,0:T(2,128)S(1)}, s32[8,2,512]{2,1,0:T(2,128)}, u32[]{:S(2)}) copy-start(s32[8,2,512]{2,1,0:T(2,128)} %cloud_ref.1) | copy-start | bytes 98308
  65.9 16.5 %collective-permute-start.3 = (bf16[768,384]{1,0:T(8,128)(2,1)S(1)}, bf16[768,384]{1,0:T(8,128)(2,1)S(1)}, u32[]{:S(2)}, u32[]{:S(2)}) collective-permute-start(bf16[768,384]{1,0:T(8,128)(2,1)S(1)} %get-tuple-element.12), channel_id=1, source_target_pairs={{0,2},{2,0},{1,3},{3,1},{4,6},{6,4},{5,7},{7,5},{8,10},{10,8},{9,1... | collective-permute-start | bytes 1769480 | tf_op jit(solution)/shard_map/ppermute | solution.py:330
  67.2 15.2 %collective-permute-start.2 = (f32[64,384]{1,0:T(8,128)S(1)}, f32[64,384]{1,0:T(8,128)S(1)}, u32[]{:S(2)}, u32[]{:S(2)}) collective-permute-start(f32[64,384]{1,0:T(8,128)S(1)} %get-tuple-element.59), channel_id=1, source_target_pairs={{0,2},{2,0},{1,3},{3,1},{4,6},{6,4},{5,7},{7,5},{8,10},{10,8},{9,1... | collective-permute-start | bytes 294920 | tf_op jit(solution)/shard_map/ppermute | solution.py:329
  68.9 13.6 %copy-start.1 = (bf16[4,64,128]{2,1,0:T(8,128)(2,1)S(1)}, bf16[4,64,128]{2,1,0:T(8,128)(2,1)}, u32[]{:S(2)}) copy-start(bf16[4,64,128]{2,1,0:T(8,128)(2,1)} %param.26) | copy-start | bytes 196612
  82.6 11.9 %copy-start.3 = (bf16[20,64]{1,0:T(8,128)(2,1)S(1)}, bf16[20,64]{1,0:T(8,128)(2,1)}, u32[]{:S(2)}) copy-start(bf16[20,64]{1,0:T(8,128)(2,1)} %cls_ref.1) | copy-start | bytes 7684
  83.5 6.6 %collective-permute-start.4 = (bf16[256,384]{1,0:T(8,128)(2,1)S(1)}, bf16[256,384]{1,0:T(8,128)(2,1)S(1)}, u32[]{:S(2)}, u32[]{:S(2)}) collective-permute-start(bf16[256,384]{1,0:T(8,128)(2,1)S(1)} %get-tuple-element.10), channel_id=1, source_target_pairs={{0,1},{1,4},{4,5},{5,8},{8,9},{9,12},{12,13},{2,3},{3,6},{6,7},{7,... | collective-permute-start | bytes 589832 | tf_op jit(solution)/shard_map/ppermute | solution.py:233
  87.5 7.0 %collective-permute-start.5 = (bf16[256,384]{1,0:T(8,128)(2,1)S(1)}, bf16[256,384]{1,0:T(8,128)(2,1)S(1)}, u32[]{:S(2)}, u32[]{:S(2)}) collective-permute-start(bf16[256,384]{1,0:T(8,128)(2,1)S(1)} %get-tuple-element.9), channel_id=1, source_target_pairs={{1,0},{4,1},{5,4},{8,5},{9,8},{12,9},{13,12},{3,2},{6,3},{7,6},{10... | collective-permute-start | bytes 589832 | tf_op jit(solution)/shard_map/ppermute | solution.py:233

commit v2 on v1

--- a/solution.py
+++ b/solution.py
@@ -37,7 +37,7 @@
 COL = ((1, 2, 0, None), (0, 1, None, 2))
 
 
-def paired(w, order):
+def paired(tap, order):
     lines = []
     for ro in range(2):
         for po in range(2):
@@ -47,26 +47,70 @@
                 for v, lo, hi in order:
                     b = COL[po][v]
                     if b is None or not 0 <= a < 3:
-                        line.append(jnp.zeros((w.shape[1], hi - lo), w.dtype))
+                        line.append(jnp.zeros((tap[0].shape[0], hi - lo), tap[0].dtype))
                     else:
-                        line.append(w[3 * a + b, :, lo:hi])
+                        line.append(tap[3 * a + b][:, lo:hi])
             lines.append(jnp.concatenate(line, axis=1))
-    return jnp.concatenate(lines, axis=0)
-
-
-def coarse_weight(w):
-    lines = []
+    return lines
+
+
+def weights_kernel(perm_f_ref, perm_c_ref, first_ref, second_ref, down_ref, coarse_ref, key_ref, out_ref, dec_ref,
+                   perm_k_ref, w1_ref, w2_ref, wd_ref, wc_ref, kw_ref, wo_ref, wdec_ref):
+    fine_ch = second_ref.shape[1]
+    coarse_ch = coarse_ref.shape[1]
+    bands = first_ref.shape[2]
+    perm_f, perm_c = perm_f_ref[...], perm_c_ref[...]
+
+    def right(w, perm):
+        return lax.dot_general(w, perm, (((1,), (1,)), ((), ())), preferred_element_type=F32)
+
+    row = lax.broadcasted_iota(jnp.int32, (bands, 256), 0)
+    col = lax.broadcasted_iota(jnp.int32, (bands, 256), 1)
     for ro in range(2):
-        line = []
+        for po in range(2):
+            total = jnp.zeros((fine_ch, 256), F32)
+            for ri in range(4):
+                for v in range(4):
+                    a, b = ri - ro, COL[po][v]
+                    if b is not None and 0 <= a < 3:
+                        place = (col == row + (4 * ri + v) * 16).astype(F32).astype(BF)
+                        total = total + dot(first_ref[3 * a + b], place)
+            base = fine_ch * (2 * ro + po)
+            w1_ref[base:base + fine_ch, :] = total.astype(BF)
+    taps = [dot(perm_f, second_ref[k]) for k in range(9)]
+    for k, line in enumerate(paired(taps, [(v, 0, fine_ch) for v in range(4)])):
+        w2_ref[fine_ch * k:fine_ch * (k + 1), :] = line.astype(BF)
+    wd_ref[...] = jnp.concatenate([right(down_ref[k], perm_f) for k in range(4)], axis=1).astype(BF)
+    taps = [dot(perm_c, coarse_ref[k]).astype(BF) for k in range(9)]
+    for ro in range(2):
         for ri in range(4):
-            a = ri - ro
-            for b in (1, 0, 2):
-                if 0 <= a < 3:
-                    line.append(w[3 * a + b])
-                else:
-                    line.append(jnp.zeros(w.shape[1:], w.dtype))
-        lines.append(jnp.concatenate(line, axis=1))
-    return jnp.concatenate(lines, axis=0)
+            for v, b in enumerate((1, 0, 2)):
+                a = ri - ro
+                x = taps[3 * a + b] if 0 <= a < 3 else jnp.zeros((coarse_ch, coarse_ch), BF)
+                base = coarse_ch * (3 * ri + v)
+                wc_ref[coarse_ch * ro:coarse_ch * (ro + 1), base:base + coarse_ch] = x
+    kw = right(dot(perm_k_ref[...], key_ref[...]).astype(BF), perm_c).astype(BF)
+    nk = kw.shape[0]
+    kw_ref[...] = jnp.zeros(kw_ref.shape, BF)
+    kw_ref[:nk, :coarse_ch] = kw
+    kw_ref[nk:, coarse_ch:] = kw
+    wo_ref[...] = right(out_ref[...], perm_c).astype(BF)
+    taps = []
+    for k in range(9):
+        w = dec_ref[k]
+        taps.append(jnp.concatenate([w[:, :fine_ch].astype(F32), right(w[:, fine_ch:], perm_f)], axis=1))
+    up, skip = (0, fine_ch), (fine_ch, 2 * fine_ch)
+    order = [(0, *up), (1, *up), (0, *skip), (1, *skip), (2, *up), (2, *skip), (3, *up), (3, *skip)]
+    for k, line in enumerate(paired(taps, order)):
+        wdec_ref[fine_ch * k:fine_ch * (k + 1), :] = line.astype(BF)
+
+
+def regroup_matrix(n, heads):
+    m = np.zeros((n, n), np.float32)
+    for h in range(heads):
+        for i in range(n // heads):
+            m[i * heads + h, h * (n // heads) + i] = 1
+    return jnp.asarray(m, BF)
 
 
 def regroup(w, axis, heads):
@@ -76,7 +120,7 @@
     return jnp.swapaxes(w.reshape(shape), axis, axis + 1).reshape(w.shape)
 
 
-def encode_kernel(heads, fine_ch, coarse_ch, edge_ref, img_ref, cloud_ref, sel_ref, w1_ref, w2_ref, wd_ref, wc_ref,
+def encode_kernel(heads, fine_ch, coarse_ch, edge_ref, up_ref, img_ref, dn_ref, cloud_ref, order_ref, sel_ref, w1_ref, w2_ref, wd_ref, wc_ref,
                   kw_ref, kb_ref, q_ref, ml_ref, out_ref, xi, s1, s2, m_s, l_s, a_s, k_s):
     t = pl.program_id(0)
     half = xi.shape[1]
@@ -91,9 +135,11 @@
         k_s[...] = jnp.zeros(k_s.shape, F32)
 
     sel = sel_ref[...]
+    img = jnp.concatenate([r[0].astype(F32) for r in (up_ref, img_ref, dn_ref)], axis=0).astype(BF)
+    img = dot(order_ref[...], img).astype(BF)
     es, os = [], []
     for q in range(2 * half // 256):
-        y = dot(img_ref[0, :, 256 * q:256 * q + 256], sel)
+        y = dot(img[:, 256 * q:256 * q + 256], sel)
         es.append(y[:, :128])
         os.append(y[:, 128:])
     e = jnp.concatenate(es, axis=1)
@@ -153,8 +199,8 @@
     def _():
         for rr in range(2):
             total = l_s[rr]
-            ml_ref[heads * rr:heads * (rr + 1), :] = m_s[rr]
-            ml_ref[heads * (2 + rr):heads * (3 + rr), :] = total
+            lse = m_s[rr] + jnp.log(jnp.maximum(total, 0.5))
+            ml_ref[heads * rr:heads * (rr + 1), :] = jnp.where(total > 0.0, lse, NEG)
             inv = (1.0 / jnp.maximum(total, 0.5))[None]
             a = (a_s[rr] * inv).reshape(coarse_ch, half)
             out_ref[coarse_ch * rr:coarse_ch * (rr + 1), :] = a.astype(BF)
@@ -169,7 +215,7 @@
     for rr in range(2):
         ms = [ml_ref[d, heads * rr:heads * (rr + 1), :] for d in range(dates)]
         top = functools.reduce(jnp.maximum, ms)
-        ws = [ml_ref[d, heads * (2 + rr):heads * (3 + rr), :] * jnp.exp(ms[d] - top) for d in range(dates)]
+        ws = [jnp.exp(m - top) for m in ms]
         inv = 1.0 / functools.reduce(jnp.add, ws)
         ws = [(w * inv)[None] for w in ws]
 
@@ -246,11 +292,15 @@
     band = lax.axis_index(ROWS)
     count = lax.axis_size(ROWS)
 
-    above = neighbour_shift(images, 1)
-    below = neighbour_shift(images, -1)
-    ext = jnp.concatenate([above, images, below], axis=2)
-    ext = jnp.pad(jnp.transpose(ext, (0, 2, 1, 3)), ((0, 0), (0, 0), (0, 16 - bands), (0, 0)))
-    ext = ext.reshape(dates, 12 * 16, cols)
+    flat = images.reshape(dates, bands * rows, cols)
+    above = neighbour_shift(flat, 1)
+    below = neighbour_shift(flat, -1)
+    order = np.zeros((12 * 16, 3 * bands * rows), np.float32)
+    for k in range(3):
+        for r in range(rows):
+            for c in range(bands):
+                order[(rows * k + r) * 16 + c, (bands * k + c) * rows + r] = 1
+    order = jnp.asarray(order, BF)
 
     edges = jnp.stack([(band > 0).astype(F32), (band < count - 1).astype(F32)])
 
@@ -260,13 +310,20 @@
         sel[2 * i + 1, 128 + i] = 1
     sel = jnp.asarray(sel, BF)
 
-    w1 = paired(jnp.pad(conv_first, ((0, 0), (0, 0), (0, 16 - bands))), [(v, 0, 16) for v in range(4)])
-    w2 = paired(regroup(conv_second, 1, heads), [(v, 0, fine_ch) for v in range(4)])
-    wd = jnp.transpose(regroup(conv_down, 2, heads), (1, 0, 2)).reshape(coarse_ch, 4 * fine_ch)
-    wc = coarse_weight(regroup(conv_coarse, 1, heads))
-    kw = regroup(regroup(key_weight, 0, heads), 1, heads)
-    zero = jnp.zeros_like(kw)
-    kw2 = jnp.concatenate([jnp.concatenate([kw, zero], 1), jnp.concatenate([zero, kw], 1)], 0)
+    nk = 2 * heads * key_size
+    n = 4 * fine_ch
+    shapes = [(n, 256), (n, 16 * fine_ch), (coarse_ch, n), (2 * coarse_ch, 12 * coarse_ch), (nk, 2 * coarse_ch),
+              (coarse_ch, coarse_ch), (n, 8 * n)]
+    w1, w2, wd, wc, kw2, wo, wdec = pl.pallas_call(
+        weights_kernel,
+        in_specs=[VMEM] * 10,
+        out_specs=[VMEM] * 7,
+        out_shape=[jax.ShapeDtypeStruct(shape, BF) for shape in shapes],
+        compiler_params=pltpu.CompilerParams(vmem_limit_bytes=48 * 1024 * 1024),
+        cost_estimate=pl.CostEstimate(flops=10**9, bytes_accessed=6 * 10**6, transcendentals=0),
+    )(regroup_matrix(fine_ch, heads), regroup_matrix(coarse_ch, heads), conv_first, conv_second, conv_down,
+      conv_coarse, key_weight, out_weight, dec_weight, regroup_matrix(heads * key_size, heads))
+
     half_ch = coarse_ch // 2
     freqs = jnp.power(1000.0, -2.0 * jnp.arange(half_ch, dtype=F32) / coarse_ch)
     angles = day_of_year.astype(F32)[:, None] * freqs[None, :]
@@ -277,7 +334,6 @@
     qv = jnp.transpose(query_weight).reshape(-1)
     qv = jnp.concatenate([qv, qv])[:, None]
 
-    nk = 2 * heads * key_size
     total = 2 * coarse_ch + 8 * fine_ch
     const = lambda *shape: pl.BlockSpec(shape, lambda t: (0,) * len(shape))
     ml, ab = pl.pallas_call(
@@ -285,8 +341,9 @@
         grid=(dates,),
         in_specs=[
             SMEM,
-            pl.BlockSpec((1, 192, cols), lambda t: (t, 0, 0)),
+            *[pl.BlockSpec((1, bands * rows, cols), lambda t: (t, 0, 0))] * 3,
             pl.BlockSpec((1, 2, half), lambda t: (t, 0, 0)),
+            const(*order.shape),
             const(256, 256),
             const(*w1.shape),
             const(*w2.shape),
@@ -296,8 +353,8 @@
             pl.BlockSpec((1, nk, 1), lambda t: (t, 0, 0)),
             const(nk, 1),
         ],
-        out_specs=[const(4 * heads, half), const(total, half)],
-        out_shape=[jax.ShapeDtypeStruct((4 * heads, half), F32), jax.ShapeDtypeStruct((total, half), BF)],
+        out_specs=[const(2 * heads, half), const(total, half)],
+        out_shape=[jax.ShapeDtypeStruct((2 * heads, half), F32), jax.ShapeDtypeStruct((total, half), BF)],
         scratch_shapes=[
             pltpu.VMEM((12 * 64, half), BF),
             pltpu.VMEM((40 * fine_ch, half), BF),
@@ -308,7 +365,7 @@
             pltpu.VMEM((2, 4 * fine_ch // heads, heads, half), F32),
         ],
         compiler_params=pltpu.CompilerParams(vmem_limit_bytes=48 * 1024 * 1024),
-    )(edges, ext, clouds, sel, w1, w2, wd, wc, kw2, kb, qv)
+    )(edges, above, flat, below, clouds, order, sel, w1, w2, wd, wc, kw2, kb, qv)
 
     per = half // groups
     spans = []
@@ -334,15 +391,10 @@
         out_specs=VMEM,
         out_shape=jax.ShapeDtypeStruct((rows * 4 * fine_ch, width), BF),
         compiler_params=pltpu.CompilerParams(vmem_limit_bytes=48 * 1024 * 1024),
-    )(jnp.stack(mls), jnp.stack(abs_), regroup(out_weight, 1, heads), up_weight.reshape(4 * fine_ch, coarse_ch))
-
-    n = 4 * fine_ch
+    )(jnp.stack(mls), jnp.stack(abs_), wo, up_weight.reshape(4 * fine_ch, coarse_ch))
+
     top = neighbour_shift(joined[-n:], 1)
     low = neighbour_shift(joined[:n], -1)
-    dec = jnp.concatenate([dec_weight[:, :, :fine_ch], regroup(dec_weight[:, :, fine_ch:], 2, heads)], axis=2)
-    up_part, skip_part = (0, fine_ch), (fine_ch, 2 * fine_ch)
-    wdec = paired(dec, [(0, *up_part), (1, *up_part), (0, *skip_part), (1, *skip_part),
-                        (2, *up_part), (2, *skip_part), (3, *up_part), (3, *skip_part)])
     offset = (me * per - starts[me]).astype(jnp.int32).reshape(1)
     return pl.pallas_call(
         functools.partial(decode_kernel, fine_ch),

time: 98.3 us -> 88.1 us (0.90)
  local copies, waits for them, and re-layouts: 22.1 us -> 12.2 us
  other arithmetic: 4.88 us -> 0.5 us
  Pallas kernels: 39.4 us -> 41.1 us
  starting transfers between devices: 14.2 us -> 15.8 us
  waiting for transfers between devices: 16.3 us -> 17.5 us
    concatenate x13 -> x0, local copies, waits for them, and re-layouts: 4.75 us -> none  [the longest x12 4.1 us: paired(): lines.append(jnp.concatenate(line, axis=1))]
    concatenate x5 -> x0, other arithmetic: 3.01 us -> none  [the longest x3 1.83 us: paired(): return jnp.concatenate(lines, axis=0)]
    pad x1 -> x0, local copies, waits for them, and re-layouts: 2.43 us -> none  [body(): jnp.pad(jnp.transpose(ext, (0, 2, 1, 3)), ((0, 0), (0, 0), (0, 16 - bands...]
    reshape x6 -> x1, local copies, waits for them, and re-layouts: 2.37 us -> 0.08 us  [regroup(): return jnp.swapaxes(w.reshape(shape), axis, axis + 1).reshape(w.shape)]
    ppermute x4, starting transfers between devices: 12.6 us -> 14.2 us  [neighbour_shift(): return lax.ppermute(x, ROWS, pairs)]
    reshape x1, local copies, waits for them, and re-layouts: 0.11 us -> 1.55 us  [body(): flat = images.reshape(dates, bands * rows, cols)]
    transpose x1 -> x0, other arithmetic: 1.36 us -> none  [body(): jnp.transpose(ext, (0, 2, 1, 3))]
    ppermute x1, waiting for transfers between devices: 11.4 us -> 12.6 us  [body(): mls.append(lax.ppermute(window(ml, to), 'date', pairs))]
  transfers between devices with their start and end apart: 6 -> 6, of which waited for: 3 -> 3; matrix products, arithmetic and copies ran while one was open for 22% -> 4% of each run, Pallas kernels for 0% -> 1%
where the time goes in v2:
time: 88.1 us; the launch traced here: 87.6 us
  Pallas kernels  41.1 us (47%)
  waiting for transfers between devices  17.5 us (20%)
  starting transfers between devices  15.8 us (18%)
  local copies, waits for them, and re-layouts  12.2 us (14%)
    pallas_call x1, Pallas kernels, body(): pl.pallas_call(functools.partial(encode_kernel, heads, fine_ch, coarse_ch...  36.1 us
    ppermute x4, starting transfers between devices, neighbour_shift(): return lax.ppermute(x, ROWS, pairs)  14.2 us
    ppermute x1, waiting for transfers between devices, body(): mls.append(lax.ppermute(window(ml, to), 'date', pairs))  12.6 us
    unnamed x42, local copies, waits for them, and re-layouts  9.14 us
    ppermute x4, waiting for transfers between devices, neighbour_shift(): return lax.ppermute(x, ROWS, pairs)  4.95 us
    pallas_call x1, Pallas kernels, body(): pl.pallas_call(functools.partial(decode_kernel, fine_ch), in_specs=[SMEM]...  3.25 us
  transfers between devices with their start and end apart: 6, of which 3 were waited for; matrix products, arithmetic and copies ran while one was open for 4% of the time, Pallas kernels for 1%

profile of v2, /device:TPU:1, one launch (start us, length us, event | category | flops | bytes accessed | tf_op | source)
XLA Modules:
  0.0 87.6 jit_solution(88719578220173728)
XLA Ops:
  0.0 1.6 %reshape.25.img_ref = bf16[8,40,1024]{2,1,0:T(8,128)(2,1)S(1)} reshape(bf16[8,10,4,1024]{3,2,1,0:T(4,128)(2,1)} %param.20) | data formatting | bytes 1310720 | tf_op jit(solution)/shard_map/reshape | solution.py:295
  1.6 4.6 %collective-permute-start = (bf16[8,40,1024]{2,1,0:T(8,128)(2,1)S(1)}, bf16[8,40,1024]{2,1,0:T(8,128)(2,1)S(1)}, u32[]{:S(2)}, u32[]{:S(2)}) collective-permute-start(bf16[8,40,1024]{2,1,0:T(8,128)(2,1)S(1)} %reshape.25.img_ref), channel_id=1, source_target_pairs={{0,1},{1,4},{4,5},{5,8},{8,9},{9,12},{12,13},{2,3},{3,6},{6,7},{7,... | collective-permute-start | bytes 1966088 | tf_op jit(solution)/shard_map/ppermute | solution.py:279
  6.2 1.9 %collective-permute-start.1 = (bf16[8,40,1024]{2,1,0:T(8,128)(2,1)S(1)}, bf16[8,40,1024]{2,1,0:T(8,128)(2,1)S(1)}, u32[]{:S(2)}, u32[]{:S(2)}) collective-permute-start(bf16[8,40,1024]{2,1,0:T(8,128)(2,1)S(1)} %reshape.25.img_ref), channel_id=1, source_target_pairs={{1,0},{4,1},{5,4},{8,5},{9,8},{12,9},{13,12},{3,2},{6,3},{7,6},{10... | collective-permute-start | bytes 1966088 | tf_op jit(solution)/shard_map/ppermute | solution.py:279
  8.2 0.8 copy.32.first_ref
  9.0 0.8 copy.33.down_ref
  10.7 0.7 copy.37.q_ref
  11.5 0.9 %copy-done.1 = bf16[9,64,10]{2,1,0:T(8,128)(2,1)S(1)} copy-done((bf16[9,64,10]{2,1,0:T(8,128)(2,1)S(1)}, bf16[9,64,10]{2,1,0:T(8,128)(2,1)}, u32[]{:S(2)}) %copy-start.1) | copy-done | bytes 11544
  12.4 0.9 %copy-done.3 = bf16[4,128,64]{2,1,0:T(8,128)(2,1)S(1)} copy-done((bf16[4,128,64]{2,1,0:T(8,128)(2,1)S(1)}, bf16[4,128,64]{2,1,0:T(8,128)(2,1)}, u32[]{:S(2)}) %copy-start.3) | copy-done | bytes 65560
  13.3 1.0 %copy-done.9 = bf16[9,128,128]{2,1,0:T(8,128)(2,1)S(1)} copy-done((bf16[9,128,128]{2,1,0:T(8,128)(2,1)S(1)}, bf16[9,128,128]{2,1,0:T(8,128)(2,1)}, u32[]{:S(2)}) %copy-start.9) | copy-done | bytes 294936
  14.3 0.9 %copy-done.10 = bf16[9,64,64]{2,1,0:T(8,128)(2,1)S(1)} copy-done((bf16[9,64,64]{2,1,0:T(8,128)(2,1)S(1)}, bf16[9,64,64]{2,1,0:T(8,128)(2,1)}, u32[]{:S(2)}) %copy-start.10) | copy-done | bytes 73752
  15.2 0.9 %copy-done.11 = bf16[9,64,128]{2,1,0:T(8,128)(2,1)S(1)} copy-done((bf16[9,64,128]{2,1,0:T(8,128)(2,1)S(1)}, bf16[9,64,128]{2,1,0:T(8,128)(2,1)}, u32[]{:S(2)}) %copy-start.11) | copy-done | bytes 147480
  16.1 0.8 copy-done.12
  16.8 0.8 copy-done.13
  17.6 0.7 copy-done.14
  18.3 0.9 %shard_map.190 = (bf16[256,256]{1,0:T(8,128)(2,1)S(1)}, bf16[256,1024]{1,0:T(8,128)(2,1)S(1)}, bf16[128,256]{1,0:T(8,128)(2,1)S(1)}, bf16[256,1536]{1,0:T(8,128)...) custom-call(bf16[64,64]{1,0:T(8,128)(2,1)S(1)} %copy-done.14, ...), custom_call_target="tpu_custom_call" | custom-call | flops 1000000000 | bytes 6000000 | tf_op jit(solution)/shard_map/pallas_call | solution.py:317
  19.4 36.1 %shard_map.191 = (f32[32,512]{1,0:T(8,128)S(1)}, bf16[768,512]{1,0:T(8,128)(2,1)S(1)}) custom-call(f32[2]{0:T(128)S(1)} %add_convert_fusion.edge_ref, bf16[8,40,1024]{2,1,0:T(8,128)(2,1)S(1)} %collective-permute-done.up_ref, bf16[8,40,1024]{2,1,0:T(8,128)(2,1)S(1)} %reshape.25.img_ref, bf16[8,40,1024]{2,1,0:T(8,128)(2,1)S(1)} %collective-permute-done.1.dn_ref, ...), custom_call_target="tpu_custom_call" | custom-call | tf_op jit(solution)/shard_map/pallas_call | solution.py:339
  55.7 1.3 %collective-permute-start.3 = (bf16[768,384]{1,0:T(8,128)(2,1)S(1)}, bf16[768,384]{1,0:T(8,128)(2,1)S(1)}, u32[]{:S(2)}, u32[]{:S(2)}) collective-permute-start(bf16[768,384]{1,0:T(8,128)(2,1)S(1)} %get-tuple-element.26), channel_id=1, source_target_pairs={{0,2},{2,0},{1,3},{3,1},{4,6},{6,4},{5,7},{7,5},{8,10},{10,8},{9,1... | collective-permute-start | bytes 1769480 | tf_op jit(solution)/shard_map/ppermute | solution.py:387
  57.3 12.6 %collective-permute-done.2 = f32[32,384]{1,0:T(8,128)S(1)} collective-permute-done((f32[32,384]{1,0:T(8,128)S(1)}, f32[32,384]{1,0:T(8,128)S(1)}, u32[]{:S(2)}, u32[]{:S(2)}) %collective-permute-start.2) | collective-permute-done | bytes 49184 | tf_op jit(solution)/shard_map/ppermute | solution.py:386
  70.0 0.7 copy-done.4
  70.7 0.8 shard_map.192.mid_ref
  71.6 5.8 %collective-permute-start.4 = (bf16[256,384]{1,0:T(8,128)(2,1)S(1)}, bf16[256,384]{1,0:T(8,128)(2,1)S(1)}, u32[]{:S(2)}, u32[]{:S(2)}) collective-permute-start(bf16[256,384]{1,0:T(8,128)(2,1)S(1)} %get-tuple-element.24), channel_id=1, source_target_pairs={{0,1},{1,4},{4,5},{5,8},{8,9},{9,12},{12,13},{2,3},{3,6},{6,7},{7,... | collective-permute-start | bytes 589832 | tf_op jit(solution)/shard_map/ppermute | solution.py:279
  77.4 1.9 %collective-permute-start.5 = (bf16[256,384]{1,0:T(8,128)(2,1)S(1)}, bf16[256,384]{1,0:T(8,128)(2,1)S(1)}, u32[]{:S(2)}, u32[]{:S(2)}) collective-permute-start(bf16[256,384]{1,0:T(8,128)(2,1)S(1)} %get-tuple-element.23), channel_id=1, source_target_pairs={{1,0},{4,1},{5,4},{8,5},{9,8},{12,9},{13,12},{3,2},{6,3},{7,6},{10... | collective-permute-start | bytes 589832 | tf_op jit(solution)/shard_map/ppermute | solution.py:279
  79.9 4.4 %collective-permute-done.5.low_ref = bf16[256,384]{1,0:T(8,128)(2,1)S(1)} collective-permute-done((bf16[256,384]{1,0:T(8,128)(2,1)S(1)}, bf16[256,384]{1,0:T(8,128)(2,1)S(1)}, u32[]{:S(2)}, u32[]{:S(2)}) %collective-permute-start.5) | collective-permute-done | bytes 196640 | tf_op jit(solution)/shard_map/ppermute | solution.py:279
  84.3 3.3 %shard_map.193 = f32[20,4,512]{2,1,0:T(4,128)} custom-call(s32[1]{0:T(128)} %bitcast.off_ref, bf16[256,384]{1,0:T(8,128)(2,1)S(1)} %collective-permute-done.4.top_ref, bf16[1024,384]{1,0:T(8,128)(2,1)S(1)} %shard_map.192.mid_ref, bf16[256,384]{1,0:T(8,128)(2,1)S(1)} %collective-permute-done.5.low_ref, bf16[256,2048]{1,0:T(8,128)(2,1)S(1)} %get-tuple-element.22.wdec_ref, ...), custom_call_target="tpu_custom_call" | custom-call | tf_op jit(solution)/shard_map/pallas_call | solution.py:399
  (53 shorter events, 2.4 us)
Async XLA Ops:
  0.0 8.2 %copy-start.16 = (bf16[9,64,10]{1,2,0:T(8,128)(2,1)S(1)}, bf16[9,64,10]{1,2,0:T(8,128)(2,1)}, u32[]{:S(2)}) copy-start(bf16[9,64,10]{1,2,0:T(8,128)(2,1)} %param.23) | copy-start | bytes 34564
  0.0 9.0 %copy-start.15 = (bf16[4,128,64]{1,2,0:T(8,128)(2,1)S(1)}, bf16[4,128,64]{1,2,0:T(8,128)(2,1)}, u32[]{:S(2)}) copy-start(bf16[4,128,64]{1,2,0:T(8,128)(2,1)} %param.25) | copy-start | bytes 196612
  0.0 9.7 %copy-start.19 = (s32[8]{0:T(128)S(1)}, s32[8]{0:T(128)}, u32[]{:S(2)}) copy-start(s32[8]{0:T(128)} %param.22) | copy-start | bytes 100
  0.0 9.9 %copy-start.7 = (bf16[64,128]{1,0:T(8,128)(2,1)S(1)}, bf16[64,128]{1,0:T(8,128)(2,1)}, u32[]{:S(2)}) copy-start(bf16[64,128]{1,0:T(8,128)(2,1)} %key_ref.1) | copy-start | bytes 49156
  0.0 10.6 %copy-start.17 = (f32[16,4]{0,1:T(4,128)S(1)}, f32[16,4]{0,1:T(4,128)}, u32[]{:S(2)}) copy-start(f32[16,4]{0,1:T(4,128)} %param.28) | copy-start | bytes 772
  1.6 17.7 %collective-permute-start = (bf16[8,40,1024]{2,1,0:T(8,128)(2,1)S(1)}, bf16[8,40,1024]{2,1,0:T(8,128)(2,1)S(1)}, u32[]{:S(2)}, u32[]{:S(2)}) collective-permute-start(bf16[8,40,1024]{2,1,0:T(8,128)(2,1)S(1)} %reshape.25.img_ref), channel_id=1, source_target_pairs={{0,1},{1,4},{4,5},{5,8},{8,9},{9,12},{12,13},{2,3},{3,6},{6,7},{7,... | collective-permute-start | bytes 1966088 | tf_op jit(solution)/shard_map/ppermute | solution.py:279
  6.2 13.1 %collective-permute-start.1 = (bf16[8,40,1024]{2,1,0:T(8,128)(2,1)S(1)}, bf16[8,40,1024]{2,1,0:T(8,128)(2,1)S(1)}, u32[]{:S(2)}, u32[]{:S(2)}) collective-permute-start(bf16[8,40,1024]{2,1,0:T(8,128)(2,1)S(1)} %reshape.25.img_ref), channel_id=1, source_target_pairs={{1,0},{4,1},{5,4},{8,5},{9,8},{12,9},{13,12},{3,2},{6,3},{7,6},{10... | collective-permute-start | bytes 1966088 | tf_op jit(solution)/shard_map/ppermute | solution.py:279
  11.5 0.9 %copy-start.1 = (bf16[9,64,10]{2,1,0:T(8,128)(2,1)S(1)}, bf16[9,64,10]{2,1,0:T(8,128)(2,1)}, u32[]{:S(2)}) copy-start(bf16[9,64,10]{2,1,0:T(8,128)(2,1)} %copy.32.first_ref) | copy-start | bytes 34564
  12.4 0.9 %copy-start.3 = (bf16[4,128,64]{2,1,0:T(8,128)(2,1)S(1)}, bf16[4,128,64]{2,1,0:T(8,128)(2,1)}, u32[]{:S(2)}) copy-start(bf16[4,128,64]{2,1,0:T(8,128)(2,1)} %copy.33.down_ref) | copy-start | bytes 196612
  13.3 1.0 %copy-start.9 = (bf16[9,128,128]{2,1,0:T(8,128)(2,1)S(1)}, bf16[9,128,128]{2,1,0:T(8,128)(2,1)}, u32[]{:S(2)}) copy-start(bf16[9,128,128]{2,1,0:T(8,128)(2,1)} %coarse_ref.1) | copy-start | bytes 884740
  14.3 0.9 %copy-start.10 = (bf16[9,64,64]{2,1,0:T(8,128)(2,1)S(1)}, bf16[9,64,64]{2,1,0:T(8,128)(2,1)}, u32[]{:S(2)}) copy-start(bf16[9,64,64]{2,1,0:T(8,128)(2,1)} %second_ref.1) | copy-start | bytes 221188
  15.2 0.9 %copy-start.11 = (bf16[9,64,128]{2,1,0:T(8,128)(2,1)S(1)}, bf16[9,64,128]{2,1,0:T(8,128)(2,1)}, u32[]{:S(2)}) copy-start(bf16[9,64,128]{2,1,0:T(8,128)(2,1)} %dec_ref.1) | copy-start | bytes 442372
  16.1 0.8 copy-start.12
  18.3 1.0 %copy-start = (f32[128,1]{1,0:T(8,128)S(1)}, f32[128,1]{1,0:T(8,128)}, u32[]{:S(2)}) copy-start(f32[128,1]{1,0:T(8,128)} %copy.37.q_ref) | copy-start | bytes 1540
  18.3 1.0 %copy-start.2 = (bf16[256,256]{1,0:T(8,128)(2,1)S(1)}, bf16[256,256]{1,0:T(8,128)(2,1)}, u32[]{:S(2)}) copy-start(bf16[256,256]{1,0:T(8,128)(2,1)} %constant.44.clone.sel_ref) | copy-start | bytes 393220
  18.3 1.0 %copy-start.5 = (bf16[192,120]{1,0:T(8,128)(2,1)S(1)}, bf16[192,120]{1,0:T(8,128)(2,1)}, u32[]{:S(2)}) copy-start(bf16[192,120]{1,0:T(8,128)(2,1)} %constant.43.clone.order_ref) | copy-start | bytes 138244
  18.3 1.0 %copy-start.6 = (s32[8,2,512]{2,1,0:T(2,128)S(1)}, s32[8,2,512]{2,1,0:T(2,128)}, u32[]{:S(2)}) copy-start(s32[8,2,512]{2,1,0:T(2,128)} %cloud_ref.1) | copy-start | bytes 98308
  55.7 14.2 %collective-permute-start.3 = (bf16[768,384]{1,0:T(8,128)(2,1)S(1)}, bf16[768,384]{1,0:T(8,128)(2,1)S(1)}, u32[]{:S(2)}, u32[]{:S(2)}) collective-permute-start(bf16[768,384]{1,0:T(8,128)(2,1)S(1)} %get-tuple-element.26), channel_id=1, source_target_pairs={{0,2},{2,0},{1,3},{3,1},{4,6},{6,4},{5,7},{7,5},{8,10},{10,8},{9,1... | collective-permute-start | bytes 1769480 | tf_op jit(solution)/shard_map/ppermute | solution.py:387
  57.0 12.9 %collective-permute-start.2 = (f32[32,384]{1,0:T(8,128)S(1)}, f32[32,384]{1,0:T(8,128)S(1)}, u32[]{:S(2)}, u32[]{:S(2)}) collective-permute-start(f32[32,384]{1,0:T(8,128)S(1)} %get-tuple-element.28), channel_id=1, source_target_pairs={{0,2},{2,0},{1,3},{3,1},{4,6},{6,4},{5,7},{7,5},{8,10},{10,8},{9,1... | collective-permute-start | bytes 147464 | tf_op jit(solution)/shard_map/ppermute | solution.py:386
  69.9 0.8 copy-start.4
  70.7 8.6 %copy-start.18 = (f32[20]{0:T(128)S(1)}, f32[20]{0:T(128)}, u32[]{:S(2)}) copy-start(f32[20]{0:T(128)} %param.33) | copy-start | bytes 244
  70.7 13.6 %copy-start.8 = (bf16[20,64]{1,0:T(8,128)(2,1)S(1)}, bf16[20,64]{1,0:T(8,128)(2,1)}, u32[]{:S(2)}) copy-start(bf16[20,64]{1,0:T(8,128)(2,1)} %cls_ref.1) | copy-start | bytes 7684
  71.6 8.4 %collective-permute-start.4 = (bf16[256,384]{1,0:T(8,128)(2,1)S(1)}, bf16[256,384]{1,0:T(8,128)(2,1)S(1)}, u32[]{:S(2)}, u32[]{:S(2)}) collective-permute-start(bf16[256,384]{1,0:T(8,128)(2,1)S(1)} %get-tuple-element.24), channel_id=1, source_target_pairs={{0,1},{1,4},{4,5},{5,8},{8,9},{9,12},{12,13},{2,3},{3,6},{6,7},{7,... | collective-permute-start | bytes 589832 | tf_op jit(solution)/shard_map/ppermute | solution.py:279
  77.4 7.0 %collective-permute-start.5 = (bf16[256,384]{1,0:T(8,128)(2,1)S(1)}, bf16[256,384]{1,0:T(8,128)(2,1)S(1)}, u32[]{:S(2)}, u32[]{:S(2)}) collective-permute-start(bf16[256,384]{1,0:T(8,128)(2,1)S(1)} %get-tuple-element.23), channel_id=1, source_target_pairs={{1,0},{4,1},{5,4},{8,5},{9,8},{12,9},{13,12},{3,2},{6,3},{7,6},{10... | collective-permute-start | bytes 589832 | tf_op jit(solution)/shard_map/ppermute | solution.py:279
  (2 other events, 1.5 us)

commit v3 on v2

--- a/solution.py
+++ b/solution.py
@@ -54,12 +54,12 @@
     return lines
 
 
-def weights_kernel(perm_f_ref, perm_c_ref, first_ref, second_ref, down_ref, coarse_ref, key_ref, out_ref, dec_ref,
-                   perm_k_ref, w1_ref, w2_ref, wd_ref, wc_ref, kw_ref, wo_ref, wdec_ref):
+def weights_kernel(heads, first_ref, second_ref, down_ref, coarse_ref, key_ref, out_ref, dec_ref, w1_ref, w2_ref, wd_ref, wc_ref, kw_ref, wo_ref, wdec_ref):
     fine_ch = second_ref.shape[1]
     coarse_ch = coarse_ref.shape[1]
     bands = first_ref.shape[2]
-    perm_f, perm_c = perm_f_ref[...], perm_c_ref[...]
+    perm_f, perm_c = regroup_matrix(fine_ch, heads), regroup_matrix(coarse_ch, heads)
+    perm_k = regroup_matrix(key_ref.shape[0], heads)
 
     def right(w, perm):
         return lax.dot_general(w, perm, (((1,), (1,)), ((), ())), preferred_element_type=F32)
@@ -89,7 +89,7 @@
                 x = taps[3 * a + b] if 0 <= a < 3 else jnp.zeros((coarse_ch, coarse_ch), BF)
                 base = coarse_ch * (3 * ri + v)
                 wc_ref[coarse_ch * ro:coarse_ch * (ro + 1), base:base + coarse_ch] = x
-    kw = right(dot(perm_k_ref[...], key_ref[...]).astype(BF), perm_c).astype(BF)
+    kw = right(dot(perm_k, key_ref[...]).astype(BF), perm_c).astype(BF)
     nk = kw.shape[0]
     kw_ref[...] = jnp.zeros(kw_ref.shape, BF)
     kw_ref[:nk, :coarse_ch] = kw
@@ -106,11 +106,10 @@
 
 
 def regroup_matrix(n, heads):
-    m = np.zeros((n, n), np.float32)
-    for h in range(heads):
-        for i in range(n // heads):
-            m[i * heads + h, h * (n // heads) + i] = 1
-    return jnp.asarray(m, BF)
+    row = lax.broadcasted_iota(jnp.int32, (n, n), 0)
+    col = lax.broadcasted_iota(jnp.int32, (n, n), 1)
+    want = lax.rem(row, heads) * (n // heads) + lax.div(row, heads)
+    return (col == want).astype(F32).astype(BF)
 
 
 def regroup(w, axis, heads):
@@ -209,54 +208,128 @@
             out_ref[base:base + 4 * fine_ch, :] = k.astype(BF)
 
 
-def combine_kernel(heads, fine_ch, coarse_ch, ml_ref, ab_ref, wo_ref, wu_ref, out_ref):
-    dates = ml_ref.shape[0]
-    width = ml_ref.shape[2]
+def tail_kernel(heads, fine_ch, coarse_ch, groups, count, starts, per, ml_ref, ab_ref, wo_ref, wu_ref, wdec_ref,
+                cls_ref, bias_ref, out_ref, ml_in, ab_in, edge_out, edge_in, s3, send, recv, edge_send, edge_recv):
+    width = ab_in.shape[2]
+    n = 4 * fine_ch
+    rows = out_ref.shape[1]
+    me = lax.axis_index("date")
+    sides = lax.axis_size("row")
+    band = lax.axis_index("tile") * sides + lax.axis_index("row")
+    mesh_id = pl.DeviceIdType.MESH
+
+    def start_of(k):
+        at = starts[0]
+        for j in range(1, groups):
+            at = at + (starts[j] - starts[j - 1]) * ((k + groups - j) // groups)
+        return pl.multiple_of(at, 128)
+
+    def beside(step):
+        other = band + step
+        return {"tile": other // sides, "row": other % sides}
+
+    barrier = pltpu.get_barrier_semaphore()
+    for step in range(1, groups):
+        pl.semaphore_signal(barrier, inc=1, device_id={"date": (me + step) % groups}, device_id_type=mesh_id)
+
+    @pl.when(band > 0)
+    def _():
+        pl.semaphore_signal(barrier, inc=1, device_id=beside(-1), device_id_type=mesh_id)
+
+    @pl.when(band < count - 1)
+    def _():
+        pl.semaphore_signal(barrier, inc=1, device_id=beside(1), device_id_type=mesh_id)
+
+    pl.semaphore_wait(barrier, groups - 1 + (band + count - 1) // count + (2 * count - 2 - band) // count)
+
+    copies = []
+    for step in range(1, groups):
+        to = (me + step) % groups
+        cols = pl.ds(start_of(to), width)
+        for kind, (src, dst) in enumerate(((ml_ref, ml_in), (ab_ref, ab_in))):
+            at = 2 * (step - 1) + kind
+            copies.append(pltpu.make_async_remote_copy(
+                src_ref=src.at[:, cols], dst_ref=dst.at[step - 1], send_sem=send.at[at], recv_sem=recv.at[at],
+                device_id={"date": to}, device_id_type=mesh_id))
+            copies[-1].start()
+    mine = start_of(me)
+    cols = pl.ds(mine, width)
+    src = lax.broadcasted_iota(jnp.int32, (2 * width, out_ref.shape[2]), 0)
+    dst = lax.broadcasted_iota(jnp.int32, (2 * width, out_ref.shape[2]), 1)
+    pick = src == me * per - mine + lax.shift_right_logical(dst, 1) + (dst & 1) * width
+    pick = pick.astype(F32).astype(BF)
+    for copy in copies:
+        copy.wait()
+
+    def put(k, x):
+        base = 2 * n * k
+        half = 2 * fine_ch
+        s3[base:base + n, :] = x
+        x = x.astype(F32).reshape(2, 2, fine_ch, width)
+        s3[base + n:base + n + half, :] = from_left(x[:, 1].reshape(half, width)).astype(BF)
+        s3[base + n + half:base + 2 * n, :] = from_right(x[:, 0].reshape(half, width)).astype(BF)
+
+    joined = []
     for rr in range(2):
-        ms = [ml_ref[d, heads * rr:heads * (rr + 1), :] for d in range(dates)]
+        head = slice(heads * rr, heads * (rr + 1))
+        ms = [ml_ref[head, cols]] + [ml_in[d, head, :] for d in range(groups - 1)]
         top = functools.reduce(jnp.maximum, ms)
         ws = [jnp.exp(m - top) for m in ms]
         inv = 1.0 / functools.reduce(jnp.add, ws)
         ws = [(w * inv)[None] for w in ws]
 
         def mix(base, size):
-            parts = [
-                ws[d] * ab_ref[d, base:base + size, :].reshape(-1, heads, width).astype(F32) for d in range(dates)
-            ]
+            parts = [ab_ref[base:base + size, cols]] + [ab_in[d, base:base + size, :] for d in range(groups - 1)]
+            parts = [w * x.reshape(-1, heads, width).astype(F32) for w, x in zip(ws, parts)]
             return functools.reduce(jnp.add, parts).reshape(size, width).astype(BF)
 
         agg = mix(coarse_ch * rr, coarse_ch)
-        skip = mix(2 * coarse_ch + 4 * fine_ch * rr, 4 * fine_ch)
+        skip = mix(2 * coarse_ch + n * rr, n)
         co = act(dot(wo_ref[...], agg)[None])[0].astype(BF)
         up = dot(wu_ref[...], co).astype(BF)
-        n = 2 * fine_ch
+        half = 2 * fine_ch
         for a in range(2):
-            base = 2 * n * (2 * rr + a)
-            out_ref[base:base + n, :] = up[n * a:n * (a + 1)]
-            out_ref[base + n:base + 2 * n, :] = skip[n * a:n * (a + 1)]
-
-
-def decode_kernel(fine_ch, off_ref, top_ref, mid_ref, low_ref, wdec_ref, cls_ref, bias_ref, out_ref, s3):
-    width = s3.shape[1]
-    n = 4 * fine_ch
-    rows = mid_ref.shape[0] // n
-    for k in range(rows + 2):
-        if k == 0:
-            x = top_ref[...]
-        elif k == rows + 1:
-            x = low_ref[...]
-        else:
-            x = mid_ref[n * (k - 1):n * k, :]
-        base = 2 * n * k
-        s3[base:base + n, :] = x
-        x = x.astype(F32).reshape(2, 2, fine_ch, width)
-        half = 2 * fine_ch
-        s3[base + n:base + n + half, :] = from_left(x[:, 1].reshape(half, width)).astype(BF)
-        s3[base + n + half:base + 2 * n, :] = from_right(x[:, 0].reshape(half, width)).astype(BF)
-    share = out_ref.shape[2]
-    src = lax.broadcasted_iota(jnp.int32, (2 * width, share), 0)
-    dst = lax.broadcasted_iota(jnp.int32, (2 * width, share), 1)
-    pick = (src == off_ref[0] + lax.shift_right_logical(dst, 1) + (dst & 1) * width).astype(F32).astype(BF)
+            joined.append(jnp.concatenate([up[half * a:half * (a + 1)], skip[half * a:half * (a + 1)]], axis=0))
+    edge_out[0] = joined[0]
+    edge_out[1] = joined[rows - 1]
+    above = pltpu.make_async_remote_copy(
+        src_ref=edge_out.at[0], dst_ref=edge_in.at[1], send_sem=edge_send.at[0], recv_sem=edge_recv.at[1],
+        device_id=beside(-1), device_id_type=mesh_id)
+    below = pltpu.make_async_remote_copy(
+        src_ref=edge_out.at[1], dst_ref=edge_in.at[0], send_sem=edge_send.at[1], recv_sem=edge_recv.at[0],
+        device_id=beside(1), device_id_type=mesh_id)
+
+    @pl.when(band > 0)
+    def _():
+        above.start()
+
+    @pl.when(band < count - 1)
+    def _():
+        below.start()
+
+    for k, x in enumerate(joined):
+        put(k + 1, x)
+
+    @pl.when(band > 0)
+    def _():
+        above.wait_send()
+        below.wait_recv()
+
+    @pl.when(band == 0)
+    def _():
+        edge_in[0] = jnp.zeros((n, width), BF)
+
+    @pl.when(band < count - 1)
+    def _():
+        below.wait_send()
+        above.wait_recv()
+
+    @pl.when(band == count - 1)
+    def _():
+        edge_in[1] = jnp.zeros((n, width), BF)
+
+    put(0, edge_in[0])
+    put(rows + 1, edge_in[1])
     for g in range(rows // 2):
         y = dot(wdec_ref[...], s3[4 * n * g:4 * n * g + 8 * n, :])
         y = act(y.reshape(4, fine_ch, width)).astype(BF)
@@ -288,7 +361,6 @@
     heads, key_size = query_weight.shape
     classes = cls_weight.shape[0]
     groups = lax.axis_size("date")
-    me = lax.axis_index("date")
     band = lax.axis_index(ROWS)
     count = lax.axis_size(ROWS)
 
@@ -312,17 +384,19 @@
 
     nk = 2 * heads * key_size
     n = 4 * fine_ch
+    const = lambda *shape: pl.BlockSpec(shape, lambda t: (0,) * len(shape))
+    raw = (conv_first, conv_second, conv_down, conv_coarse, key_weight, out_weight, dec_weight)
     shapes = [(n, 256), (n, 16 * fine_ch), (coarse_ch, n), (2 * coarse_ch, 12 * coarse_ch), (nk, 2 * coarse_ch),
               (coarse_ch, coarse_ch), (n, 8 * n)]
     w1, w2, wd, wc, kw2, wo, wdec = pl.pallas_call(
-        weights_kernel,
-        in_specs=[VMEM] * 10,
-        out_specs=[VMEM] * 7,
+        functools.partial(weights_kernel, heads),
+        grid=(1,),
+        in_specs=[const(*w.shape) for w in raw],
+        out_specs=[const(*shape) for shape in shapes],
         out_shape=[jax.ShapeDtypeStruct(shape, BF) for shape in shapes],
         compiler_params=pltpu.CompilerParams(vmem_limit_bytes=48 * 1024 * 1024),
         cost_estimate=pl.CostEstimate(flops=10**9, bytes_accessed=6 * 10**6, transcendentals=0),
-    )(regroup_matrix(fine_ch, heads), regroup_matrix(coarse_ch, heads), conv_first, conv_second, conv_down,
-      conv_coarse, key_weight, out_weight, dec_weight, regroup_matrix(heads * key_size, heads))
+    )(*raw)
 
     half_ch = coarse_ch // 2
     freqs = jnp.power(1000.0, -2.0 * jnp.arange(half_ch, dtype=F32) / coarse_ch)
@@ -335,7 +409,6 @@
     qv = jnp.concatenate([qv, qv])[:, None]
 
     total = 2 * coarse_ch + 8 * fine_ch
-    const = lambda *shape: pl.BlockSpec(shape, lambda t: (0,) * len(shape))
     ml, ab = pl.pallas_call(
         functools.partial(encode_kernel, heads, fine_ch, coarse_ch),
         grid=(dates,),
@@ -374,36 +447,26 @@
         hi = min(half // 128 - 1, (k * per + per) // 128)
         spans.append((lo, hi))
     width = max(hi - lo + 1 for lo, hi in spans) * 128
-    starts = jnp.asarray([min(lo * 128, half - width) for lo, hi in spans], jnp.int32)
-
-    def window(x, k):
-        return lax.dynamic_slice_in_dim(x, starts[k], width, 1)
-
-    mls, abs_ = [window(ml, me)], [window(ab, me)]
-    for step in range(1, groups):
-        to = lax.rem(me + step, groups)
-        pairs = [(i, (i + step) % groups) for i in range(groups)]
-        mls.append(lax.ppermute(window(ml, to), "date", pairs))
-        abs_.append(lax.ppermute(window(ab, to), "date", pairs))
-    joined = pl.pallas_call(
-        functools.partial(combine_kernel, heads, fine_ch, coarse_ch),
-        in_specs=[VMEM] * 4,
-        out_specs=VMEM,
-        out_shape=jax.ShapeDtypeStruct((rows * 4 * fine_ch, width), BF),
-        compiler_params=pltpu.CompilerParams(vmem_limit_bytes=48 * 1024 * 1024),
-    )(jnp.stack(mls), jnp.stack(abs_), wo, up_weight.reshape(4 * fine_ch, coarse_ch))
-
-    top = neighbour_shift(joined[-n:], 1)
-    low = neighbour_shift(joined[:n], -1)
-    offset = (me * per - starts[me]).astype(jnp.int32).reshape(1)
+    starts = [min(lo * 128, half - width) for lo, hi in spans]
     return pl.pallas_call(
-        functools.partial(decode_kernel, fine_ch),
-        in_specs=[SMEM] + [VMEM] * 6,
+        functools.partial(tail_kernel, heads, fine_ch, coarse_ch, groups, count, starts, per),
+        in_specs=[VMEM] * 7,
         out_specs=VMEM,
         out_shape=jax.ShapeDtypeStruct((classes, rows, cols // groups), F32),
-        scratch_shapes=[pltpu.VMEM(((rows + 2) * 2 * n, width), BF)],
-        compiler_params=pltpu.CompilerParams(vmem_limit_bytes=48 * 1024 * 1024),
-    )(offset, top, joined, low, wdec, cls_weight, cls_bias[:, None])
+        scratch_shapes=[
+            pltpu.VMEM((groups - 1, 2 * heads, width), F32),
+            pltpu.VMEM((groups - 1, total, width), BF),
+            pltpu.VMEM((2, n, width), BF),
+            pltpu.VMEM((2, n, width), BF),
+            pltpu.VMEM(((rows + 2) * 2 * n, width), BF),
+            pltpu.SemaphoreType.DMA((2 * (groups - 1),)),
+            pltpu.SemaphoreType.DMA((2 * (groups - 1),)),
+            pltpu.SemaphoreType.DMA((2,)),
+            pltpu.SemaphoreType.DMA((2,)),
+        ],
+        compiler_params=pltpu.CompilerParams(
+            vmem_limit_bytes=48 * 1024 * 1024, collective_id=0, has_side_effects=True),
+    )(ml, ab, wo, up_weight.reshape(n, coarse_ch), wdec, cls_weight, cls_bias[:, None])
 
 
 def solution(mesh):

time: 88.1 us -> 80.8 us (0.917)
  Pallas kernels: 41.1 us -> 62 us
  waiting for transfers between devices: 17.5 us -> 5.11 us
  starting transfers between devices: 15.8 us -> 6.52 us
  local copies, waits for them, and re-layouts: 12.2 us -> 6.12 us
    pallas_call x3 -> x2, Pallas kernels: 4.97 us -> 25.7 us  [the longest x1 24.8 us: body(): pl.pallas_call(functools.partial(tail_kernel, heads, fine_ch, coarse_ch,...]
    ppermute x2 -> x0, waiting for transfers between devices: 12.6 us -> none  [the longest x1 12.6 us: body(): mls.append(lax.ppermute(window(ml, to), 'date', pairs))]
    ppermute x4 -> x2, starting transfers between devices: 14.2 us -> 6.52 us  [neighbour_shift(): return lax.ppermute(x, ROWS, pairs)]
    unnamed x42 -> x33, local copies, waits for them, and re-layouts: 9.14 us -> 3.94 us
    ppermute x2 -> x0, starting transfers between devices: 1.6 us -> none  [the longest x1 1.28 us: body(): abs_.append(lax.ppermute(window(ab, to), 'date', pairs))]
    ppermute x4 -> x2, waiting for transfers between devices: 4.95 us -> 5.11 us  [neighbour_shift(): return lax.ppermute(x, ROWS, pairs)]
  transfers between devices with their start and end apart: 6 -> 2, of which waited for: 3 -> 2; matrix products, arithmetic and copies ran while one was open for 4% -> 2% of each run, Pallas kernels for 1% -> 1%
where the time goes in v3:
time: 80.8 us; the launch traced here: 80.5 us
  Pallas kernels  62 us (77%)
  starting transfers between devices  6.52 us (8%)
  local copies, waits for them, and re-layouts  6.12 us (8%)
  waiting for transfers between devices  5.11 us (6%)
    pallas_call x1, Pallas kernels, body(): pl.pallas_call(functools.partial(encode_kernel, heads, fine_ch, coarse_ch...  36.3 us
    pallas_call x1, Pallas kernels, body(): pl.pallas_call(functools.partial(tail_kernel, heads, fine_ch, coarse_ch,...  24.8 us
    ppermute x2, starting transfers between devices, neighbour_shift(): return lax.ppermute(x, ROWS, pairs)  6.52 us
    ppermute x2, waiting for transfers between devices, neighbour_shift(): return lax.ppermute(x, ROWS, pairs)  5.11 us
    unnamed x33, local copies, waits for them, and re-layouts  3.94 us
  transfers between devices with their start and end apart: 2, of which 2 were waited for; matrix products, arithmetic and copies ran while one was open for 2% of the time, Pallas kernels for 1%

profile of v3, /device:TPU:1, one launch (start us, length us, event | category | flops | bytes accessed | tf_op | source)
XLA Modules:
  0.0 80.5 jit_solution(15951345267431452381)
XLA Ops:
  0.0 1.5 %reshape.21.img_ref = bf16[8,40,1024]{2,1,0:T(8,128)(2,1)S(1)} reshape(bf16[8,10,4,1024]{3,2,1,0:T(4,128)(2,1)} %param.16) | data formatting | bytes 1310720 | tf_op jit(solution)/shard_map/reshape | solution.py:367
  1.5 4.6 %collective-permute-start = (bf16[8,40,1024]{2,1,0:T(8,128)(2,1)S(1)}, bf16[8,40,1024]{2,1,0:T(8,128)(2,1)S(1)}, u32[]{:S(2)}, u32[]{:S(2)}) collective-permute-start(bf16[8,40,1024]{2,1,0:T(8,128)(2,1)S(1)} %reshape.21.img_ref), channel_id=1, source_target_pairs={{0,1},{1,4},{4,5},{5,8},{8,9},{9,12},{12,13},{2,3},{3,6},{6,7},{7,... | collective-permute-start | bytes 1966088 | tf_op jit(solution)/shard_map/ppermute | solution.py:352
  6.1 1.9 %collective-permute-start.1 = (bf16[8,40,1024]{2,1,0:T(8,128)(2,1)S(1)}, bf16[8,40,1024]{2,1,0:T(8,128)(2,1)S(1)}, u32[]{:S(2)}, u32[]{:S(2)}) collective-permute-start(bf16[8,40,1024]{2,1,0:T(8,128)(2,1)S(1)} %reshape.21.img_ref), channel_id=1, source_target_pairs={{1,0},{4,1},{5,4},{8,5},{9,8},{12,9},{13,12},{3,2},{6,3},{7,6},{10... | collective-permute-start | bytes 1966088 | tf_op jit(solution)/shard_map/ppermute | solution.py:352
  8.1 0.2 copy.28.first_ref
  8.2 0.7 copy-done.10
  8.9 0.1 copy.29.down_ref
  9.1 0.6 copy-done.14
  9.7 0.1 multiply_sine_fusion
  9.8 0.2 fusion
  10.1 0.1 copy.31
  10.1 0.1 reshape.23
  10.3 0.2 copy.32.kb_ref
  10.5 0.3 copy-done.12
  10.8 0.1 reshape.24
  11.0 0.1 copy.33.q_ref
  11.1 0.7 copy-done.13
  11.8 0.1 copy.34.bias_ref
  11.9 0.9 %shard_map.154 = (bf16[256,256]{1,0:T(8,128)(2,1)S(1)}, bf16[256,1024]{1,0:T(8,128)(2,1)S(1)}, bf16[128,256]{1,0:T(8,128)(2,1)S(1)}, bf16[256,1536]{1,0:T(8,128)...) custom-call(bf16[9,64,10]{2,1,0:T(8,128)(2,1)S(1)} %copy.28.first_ref, ...), custom_call_target="tpu_custom_call" | custom-call | flops 1000000000 | bytes 6000000 | tf_op jit(solution)/shard_map/pallas_call | solution.py:391
  12.9 0.7 collective-permute-done.up_ref
  13.6 4.4 %collective-permute-done.1.dn_ref = bf16[8,40,1024]{2,1,0:T(8,128)(2,1)S(1)} collective-permute-done((bf16[8,40,1024]{2,1,0:T(8,128)(2,1)S(1)}, bf16[8,40,1024]{2,1,0:T(8,128)(2,1)S(1)}, u32[]{:S(2)}, u32[]{:S(2)}) %collective-permute-start.1) | collective-permute-done | bytes 655392 | tf_op jit(solution)/shard_map/ppermute | solution.py:352
  18.0 36.3 %shard_map.155 = (f32[32,512]{1,0:T(8,128)S(1)}, bf16[768,512]{1,0:T(8,128)(2,1)S(1)}) custom-call(f32[2]{0:T(128)S(1)} %add_convert_fusion.edge_ref, bf16[8,40,1024]{2,1,0:T(8,128)(2,1)S(1)} %collective-permute-done.up_ref, bf16[8,40,1024]{2,1,0:T(8,128)(2,1)S(1)} %reshape.21.img_ref, bf16[8,40,1024]{2,1,0:T(8,128)(2,1)S(1)} %collective-permute-done.1.dn_ref, ...), custom_call_target="tpu_custom_call" | custom-call | tf_op jit(solution)/shard_map/pallas_call | solution.py:412
  54.4 0.7 copy-done.5
  55.0 24.8 %shard_map.156 = f32[20,4,512]{2,1,0:T(4,128)S(1)} custom-call(f32[32,512]{1,0:T(8,128)S(1)} %get-tuple-element.19.ml_ref, bf16[768,512]{1,0:T(8,128)(2,1)S(1)} %get-tuple-element.20.ab_ref, bf16[128,128]{1,0:T(8,128)(2,1)S(1)} %get-tuple-element.21.wo_ref, bf16[256,128]{1,0:T(8,128)(2,1)S(1)} %bitcast.13, bf16[256,2048]{1,0:T(8,128)(2,1)S(1)} %get-tuple-element.22.wdec_ref, ...), custom_call_target="tpu_custom_call" | custom-call | tf_op jit(solution)/shard_map/pallas_call | solution.py:451
  79.8 0.7 copy.37
  (30 shorter events, 0.3 us)
Async XLA Ops:
  0.0 8.1 %copy-start.11 = (bf16[9,64,10]{1,2,0:T(8,128)(2,1)S(1)}, bf16[9,64,10]{1,2,0:T(8,128)(2,1)}, u32[]{:S(2)}) copy-start(bf16[9,64,10]{1,2,0:T(8,128)(2,1)} %param.19) | copy-start | bytes 34564
  1.5 12.1 %collective-permute-start = (bf16[8,40,1024]{2,1,0:T(8,128)(2,1)S(1)}, bf16[8,40,1024]{2,1,0:T(8,128)(2,1)S(1)}, u32[]{:S(2)}, u32[]{:S(2)}) collective-permute-start(bf16[8,40,1024]{2,1,0:T(8,128)(2,1)S(1)} %reshape.21.img_ref), channel_id=1, source_target_pairs={{0,1},{1,4},{4,5},{5,8},{8,9},{9,12},{12,13},{2,3},{3,6},{6,7},{7,... | collective-permute-start | bytes 1966088 | tf_op jit(solution)/shard_map/ppermute | solution.py:352
  6.1 11.9 %collective-permute-start.1 = (bf16[8,40,1024]{2,1,0:T(8,128)(2,1)S(1)}, bf16[8,40,1024]{2,1,0:T(8,128)(2,1)S(1)}, u32[]{:S(2)}, u32[]{:S(2)}) collective-permute-start(bf16[8,40,1024]{2,1,0:T(8,128)(2,1)S(1)} %reshape.21.img_ref), channel_id=1, source_target_pairs={{1,0},{4,1},{5,4},{8,5},{9,8},{12,9},{13,12},{3,2},{6,3},{7,6},{10... | collective-permute-start | bytes 1966088 | tf_op jit(solution)/shard_map/ppermute | solution.py:352
  8.1 0.8 %copy-start.10 = (bf16[4,128,64]{1,2,0:T(8,128)(2,1)S(1)}, bf16[4,128,64]{1,2,0:T(8,128)(2,1)}, u32[]{:S(2)}) copy-start(bf16[4,128,64]{1,2,0:T(8,128)(2,1)} %param.21) | copy-start | bytes 196612
  9.0 0.8 copy-start.4
  9.1 0.7 copy-start.14
  10.1 0.7 copy-start.12
  10.1 1.7 %copy-start.9 = (bf16[128,128]{1,0:T(8,128)(2,1)S(1)}, bf16[128,128]{1,0:T(8,128)(2,1)}, u32[]{:S(2)}) copy-start(bf16[128,128]{1,0:T(8,128)(2,1)} %out_ref.1) | copy-start | bytes 98308
  10.3 1.6 %copy-start.6 = (bf16[9,128,128]{2,1,0:T(8,128)(2,1)S(1)}, bf16[9,128,128]{2,1,0:T(8,128)(2,1)}, u32[]{:S(2)}) copy-start(bf16[9,128,128]{2,1,0:T(8,128)(2,1)} %coarse_ref.1) | copy-start | bytes 884740
  10.3 1.6 %copy-start.7 = (bf16[9,64,64]{2,1,0:T(8,128)(2,1)S(1)}, bf16[9,64,64]{2,1,0:T(8,128)(2,1)}, u32[]{:S(2)}) copy-start(bf16[9,64,64]{2,1,0:T(8,128)(2,1)} %second_ref.1) | copy-start | bytes 221188
  10.3 1.6 %copy-start.8 = (bf16[9,64,128]{2,1,0:T(8,128)(2,1)S(1)}, bf16[9,64,128]{2,1,0:T(8,128)(2,1)}, u32[]{:S(2)}) copy-start(bf16[9,64,128]{2,1,0:T(8,128)(2,1)} %dec_ref.1) | copy-start | bytes 442372
  11.1 0.7 copy-start.13
  11.9 6.1 %copy-start = (bf16[256,256]{1,0:T(8,128)(2,1)S(1)}, bf16[256,256]{1,0:T(8,128)(2,1)}, u32[]{:S(2)}) copy-start(bf16[256,256]{1,0:T(8,128)(2,1)} %constant.27.clone.sel_ref) | copy-start | bytes 393220
  11.9 6.1 %copy-start.2 = (bf16[192,120]{1,0:T(8,128)(2,1)S(1)}, bf16[192,120]{1,0:T(8,128)(2,1)}, u32[]{:S(2)}) copy-start(bf16[192,120]{1,0:T(8,128)(2,1)} %constant.26.clone.order_ref) | copy-start | bytes 138244
  11.9 6.1 %copy-start.3 = (s32[8,2,512]{2,1,0:T(2,128)S(1)}, s32[8,2,512]{2,1,0:T(2,128)}, u32[]{:S(2)}) copy-start(s32[8,2,512]{2,1,0:T(2,128)} %cloud_ref.1) | copy-start | bytes 98308
  18.0 36.3 %copy-start.1 = (bf16[4,64,128]{2,1,0:T(8,128)(2,1)S(1)}, bf16[4,64,128]{2,1,0:T(8,128)(2,1)}, u32[]{:S(2)}) copy-start(bf16[4,64,128]{2,1,0:T(8,128)(2,1)} %param.26) | copy-start | bytes 196612
  54.3 0.7 copy-start.5

commit v4 on v3

--- a/solution.py
+++ b/solution.py
@@ -209,10 +209,11 @@
 
 
 def tail_kernel(heads, fine_ch, coarse_ch, groups, count, starts, per, ml_ref, ab_ref, wo_ref, wu_ref, wdec_ref,
-                cls_ref, bias_ref, out_ref, ml_in, ab_in, edge_out, edge_in, s3, send, recv, edge_send, edge_recv):
+                cls_ref, bias_ref, out_ref, ml_in, ab_in, halo_out, halo_in, edge_out, edge_in, s3, send, recv, edge_send, edge_recv):
     width = ab_in.shape[2]
     n = 4 * fine_ch
     rows = out_ref.shape[1]
+    packed = groups == 2 and per % 128 == 0 and width == per + 128
     me = lax.axis_index("date")
     sides = lax.axis_size("row")
     band = lax.axis_index("tile") * sides + lax.axis_index("row")
@@ -246,10 +247,23 @@
     for step in range(1, groups):
         to = (me + step) % groups
         cols = pl.ds(start_of(to), width)
-        for kind, (src, dst) in enumerate(((ml_ref, ml_in), (ab_ref, ab_in))):
-            at = 2 * (step - 1) + kind
+        pairs = [(ml_ref.at[:, cols], ml_in.at[step - 1])]
+        if packed:
+            own = ab_ref.at[:, pl.ds(pl.multiple_of(per * to, 128), per)]
+            pairs.append((own, ab_in.at[0, :, pl.ds(pl.multiple_of(128 * to, 128), per)]))
+            block = ab_ref[:, pl.ds(pl.multiple_of(per - 128 + 128 * me, 128), 128)]
+            lane = lax.broadcasted_iota(jnp.int32, (16, 128), 1)
+            line = lax.broadcasted_iota(jnp.int32, (16, 128), 0)
+            mark = ((line == 0) & (lane == 127 * (1 - me))).astype(F32).astype(BF)
+            halo_out[...] = lax.dot_general(
+                mark, block, (((1,), (1,)), ((), ())), preferred_element_type=F32).astype(BF)
+            pairs.append((halo_out, halo_in))
+        else:
+            pairs.append((ab_ref.at[:, cols], ab_in.at[step - 1]))
+        for kind, (src, dst) in enumerate(pairs):
+            at = 3 * (step - 1) + kind
             copies.append(pltpu.make_async_remote_copy(
-                src_ref=src.at[:, cols], dst_ref=dst.at[step - 1], send_sem=send.at[at], recv_sem=recv.at[at],
+                src_ref=src, dst_ref=dst, send_sem=send.at[at], recv_sem=recv.at[at],
                 device_id={"date": to}, device_id_type=mesh_id))
             copies[-1].start()
     mine = start_of(me)
@@ -260,6 +274,12 @@
     pick = pick.astype(F32).astype(BF)
     for copy in copies:
         copy.wait()
+    if packed:
+        lane = lax.broadcasted_iota(jnp.int32, (16, 128), 1)
+        line = lax.broadcasted_iota(jnp.int32, (16, 128), 0)
+        mark = ((line == 0) & (lane == 127 * me)).astype(F32).astype(BF)
+        block = lax.dot_general(halo_in[...], mark, (((0,), (0,)), ((), ())), preferred_element_type=F32)
+        ab_in[0, :, pl.ds(pl.multiple_of(per * (1 - me), 128), 128)] = block.astype(BF)
 
     def put(k, x):
         base = 2 * n * k
@@ -456,11 +476,13 @@
         scratch_shapes=[
             pltpu.VMEM((groups - 1, 2 * heads, width), F32),
             pltpu.VMEM((groups - 1, total, width), BF),
+            pltpu.VMEM((16, total), BF),
+            pltpu.VMEM((16, total), BF),
             pltpu.VMEM((2, n, width), BF),
             pltpu.VMEM((2, n, width), BF),
             pltpu.VMEM(((rows + 2) * 2 * n, width), BF),
-            pltpu.SemaphoreType.DMA((2 * (groups - 1),)),
-            pltpu.SemaphoreType.DMA((2 * (groups - 1),)),
+            pltpu.SemaphoreType.DMA((3 * (groups - 1),)),
+            pltpu.SemaphoreType.DMA((3 * (groups - 1),)),
             pltpu.SemaphoreType.DMA((2,)),
             pltpu.SemaphoreType.DMA((2,)),
         ],

time: 80.8 us -> 77.6 us (0.960)
  Pallas kernels: 62 us -> 58.7 us
    pallas_call x1, Pallas kernels: 24.8 us -> 21.5 us  [body(): pl.pallas_call(functools.partial(tail_kernel, heads, fine_ch, coarse_ch,...]
where the time goes in v4:
time: 77.6 us; the launch traced here: 77.2 us
  Pallas kernels  58.7 us (76%)
  starting transfers between devices  6.52 us (8%)
  local copies, waits for them, and re-layouts  6.12 us (8%)
  waiting for transfers between devices  5.11 us (7%)
    pallas_call x1, Pallas kernels, body(): pl.pallas_call(functools.partial(encode_kernel, heads, fine_ch, coarse_ch...  36.3 us
    pallas_call x1, Pallas kernels, body(): pl.pallas_call(functools.partial(tail_kernel, heads, fine_ch, coarse_ch,...  21.5 us
    ppermute x2, starting transfers between devices, neighbour_shift(): return lax.ppermute(x, ROWS, pairs)  6.52 us
    ppermute x2, waiting for transfers between devices, neighbour_shift(): return lax.ppermute(x, ROWS, pairs)  5.11 us
    unnamed x33, local copies, waits for them, and re-layouts  3.94 us
  transfers between devices with their start and end apart: 2, of which 2 were waited for; matrix products, arithmetic and copies ran while one was open for 2% of the time, Pallas kernels for 1%

profile of v4, /device:TPU:1, one launch (start us, length us, event | category | flops | bytes accessed | tf_op | source)
XLA Modules:
  0.0 77.2 jit_solution(3285218328376846842)
XLA Ops:
  0.0 1.5 %reshape.21.img_ref = bf16[8,40,1024]{2,1,0:T(8,128)(2,1)S(1)} reshape(bf16[8,10,4,1024]{3,2,1,0:T(4,128)(2,1)} %param.16) | data formatting | bytes 1310720 | tf_op jit(solution)/shard_map/reshape | solution.py:387
  1.5 4.6 %collective-permute-start = (bf16[8,40,1024]{2,1,0:T(8,128)(2,1)S(1)}, bf16[8,40,1024]{2,1,0:T(8,128)(2,1)S(1)}, u32[]{:S(2)}, u32[]{:S(2)}) collective-permute-start(bf16[8,40,1024]{2,1,0:T(8,128)(2,1)S(1)} %reshape.21.img_ref), channel_id=1, source_target_pairs={{0,1},{1,4},{4,5},{5,8},{8,9},{9,12},{12,13},{2,3},{3,6},{6,7},{7,... | collective-permute-start | bytes 1966088 | tf_op jit(solution)/shard_map/ppermute | solution.py:372
  6.1 1.9 %collective-permute-start.1 = (bf16[8,40,1024]{2,1,0:T(8,128)(2,1)S(1)}, bf16[8,40,1024]{2,1,0:T(8,128)(2,1)S(1)}, u32[]{:S(2)}, u32[]{:S(2)}) collective-permute-start(bf16[8,40,1024]{2,1,0:T(8,128)(2,1)S(1)} %reshape.21.img_ref), channel_id=1, source_target_pairs={{1,0},{4,1},{5,4},{8,5},{9,8},{12,9},{13,12},{3,2},{6,3},{7,6},{10... | collective-permute-start | bytes 1966088 | tf_op jit(solution)/shard_map/ppermute | solution.py:372
  8.1 0.2 copy.28.first_ref
  8.2 0.7 copy-done.10
  8.9 0.1 copy.29.down_ref
  9.1 0.6 copy-done.14
  9.7 0.1 multiply_sine_fusion
  9.8 0.2 fusion
  10.1 0.1 copy.31
  10.1 0.1 reshape.23
  10.3 0.2 copy.32.kb_ref
  10.5 0.3 copy-done.12
  10.8 0.1 reshape.24
  11.0 0.1 copy.33.q_ref
  11.1 0.7 copy-done.13
  11.8 0.1 copy.34.bias_ref
  11.9 0.9 %shard_map.154 = (bf16[256,256]{1,0:T(8,128)(2,1)S(1)}, bf16[256,1024]{1,0:T(8,128)(2,1)S(1)}, bf16[128,256]{1,0:T(8,128)(2,1)S(1)}, bf16[256,1536]{1,0:T(8,128)...) custom-call(bf16[9,64,10]{2,1,0:T(8,128)(2,1)S(1)} %copy.28.first_ref, ...), custom_call_target="tpu_custom_call" | custom-call | flops 1000000000 | bytes 6000000 | tf_op jit(solution)/shard_map/pallas_call | solution.py:411
  12.9 0.7 collective-permute-done.up_ref
  13.6 4.4 %collective-permute-done.1.dn_ref = bf16[8,40,1024]{2,1,0:T(8,128)(2,1)S(1)} collective-permute-done((bf16[8,40,1024]{2,1,0:T(8,128)(2,1)S(1)}, bf16[8,40,1024]{2,1,0:T(8,128)(2,1)S(1)}, u32[]{:S(2)}, u32[]{:S(2)}) %collective-permute-start.1) | collective-permute-done | bytes 655392 | tf_op jit(solution)/shard_map/ppermute | solution.py:372
  18.0 36.3 %shard_map.155 = (f32[32,512]{1,0:T(8,128)S(1)}, bf16[768,512]{1,0:T(8,128)(2,1)S(1)}) custom-call(f32[2]{0:T(128)S(1)} %add_convert_fusion.edge_ref, bf16[8,40,1024]{2,1,0:T(8,128)(2,1)S(1)} %collective-permute-done.up_ref, bf16[8,40,1024]{2,1,0:T(8,128)(2,1)S(1)} %reshape.21.img_ref, bf16[8,40,1024]{2,1,0:T(8,128)(2,1)S(1)} %collective-permute-done.1.dn_ref, ...), custom_call_target="tpu_custom_call" | custom-call | tf_op jit(solution)/shard_map/pallas_call | solution.py:432
  54.4 0.7 copy-done.5
  55.0 21.5 %shard_map.156 = f32[20,4,512]{2,1,0:T(4,128)S(1)} custom-call(f32[32,512]{1,0:T(8,128)S(1)} %get-tuple-element.19.ml_ref, bf16[768,512]{1,0:T(8,128)(2,1)S(1)} %get-tuple-element.20.ab_ref, bf16[128,128]{1,0:T(8,128)(2,1)S(1)} %get-tuple-element.21.wo_ref, bf16[256,128]{1,0:T(8,128)(2,1)S(1)} %bitcast.13, bf16[256,2048]{1,0:T(8,128)(2,1)S(1)} %get-tuple-element.22.wdec_ref, ...), custom_call_target="tpu_custom_call" | custom-call | tf_op jit(solution)/shard_map/pallas_call | solution.py:471
  76.6 0.7 copy.37
  (30 shorter events, 0.3 us)
Async XLA Ops:
  0.0 8.1 %copy-start.11 = (bf16[9,64,10]{1,2,0:T(8,128)(2,1)S(1)}, bf16[9,64,10]{1,2,0:T(8,128)(2,1)}, u32[]{:S(2)}) copy-start(bf16[9,64,10]{1,2,0:T(8,128)(2,1)} %param.19) | copy-start | bytes 34564
  1.5 12.1 %collective-permute-start = (bf16[8,40,1024]{2,1,0:T(8,128)(2,1)S(1)}, bf16[8,40,1024]{2,1,0:T(8,128)(2,1)S(1)}, u32[]{:S(2)}, u32[]{:S(2)}) collective-permute-start(bf16[8,40,1024]{2,1,0:T(8,128)(2,1)S(1)} %reshape.21.img_ref), channel_id=1, source_target_pairs={{0,1},{1,4},{4,5},{5,8},{8,9},{9,12},{12,13},{2,3},{3,6},{6,7},{7,... | collective-permute-start | bytes 1966088 | tf_op jit(solution)/shard_map/ppermute | solution.py:372
  6.1 11.9 %collective-permute-start.1 = (bf16[8,40,1024]{2,1,0:T(8,128)(2,1)S(1)}, bf16[8,40,1024]{2,1,0:T(8,128)(2,1)S(1)}, u32[]{:S(2)}, u32[]{:S(2)}) collective-permute-start(bf16[8,40,1024]{2,1,0:T(8,128)(2,1)S(1)} %reshape.21.img_ref), channel_id=1, source_target_pairs={{1,0},{4,1},{5,4},{8,5},{9,8},{12,9},{13,12},{3,2},{6,3},{7,6},{10... | collective-permute-start | bytes 1966088 | tf_op jit(solution)/shard_map/ppermute | solution.py:372
  8.1 0.8 %copy-start.10 = (bf16[4,128,64]{1,2,0:T(8,128)(2,1)S(1)}, bf16[4,128,64]{1,2,0:T(8,128)(2,1)}, u32[]{:S(2)}) copy-start(bf16[4,128,64]{1,2,0:T(8,128)(2,1)} %param.21) | copy-start | bytes 196612
  9.0 0.8 %copy-start.4 = (bf16[64,128]{1,0:T(8,128)(2,1)S(1)}, bf16[64,128]{1,0:T(8,128)(2,1)}, u32[]{:S(2)}) copy-start(bf16[64,128]{1,0:T(8,128)(2,1)} %key_ref.1) | copy-start | bytes 49156
  9.1 0.7 copy-start.14
  10.1 0.7 copy-start.12
  10.1 1.7 %copy-start.9 = (bf16[128,128]{1,0:T(8,128)(2,1)S(1)}, bf16[128,128]{1,0:T(8,128)(2,1)}, u32[]{:S(2)}) copy-start(bf16[128,128]{1,0:T(8,128)(2,1)} %out_ref.1) | copy-start | bytes 98308
  10.3 1.6 %copy-start.6 = (bf16[9,128,128]{2,1,0:T(8,128)(2,1)S(1)}, bf16[9,128,128]{2,1,0:T(8,128)(2,1)}, u32[]{:S(2)}) copy-start(bf16[9,128,128]{2,1,0:T(8,128)(2,1)} %coarse_ref.1) | copy-start | bytes 884740
  10.3 1.6 %copy-start.7 = (bf16[9,64,64]{2,1,0:T(8,128)(2,1)S(1)}, bf16[9,64,64]{2,1,0:T(8,128)(2,1)}, u32[]{:S(2)}) copy-start(bf16[9,64,64]{2,1,0:T(8,128)(2,1)} %second_ref.1) | copy-start | bytes 221188
  10.3 1.6 %copy-start.8 = (bf16[9,64,128]{2,1,0:T(8,128)(2,1)S(1)}, bf16[9,64,128]{2,1,0:T(8,128)(2,1)}, u32[]{:S(2)}) copy-start(bf16[9,64,128]{2,1,0:T(8,128)(2,1)} %dec_ref.1) | copy-start | bytes 442372
  11.1 0.7 copy-start.13
  11.9 6.1 %copy-start = (bf16[256,256]{1,0:T(8,128)(2,1)S(1)}, bf16[256,256]{1,0:T(8,128)(2,1)}, u32[]{:S(2)}) copy-start(bf16[256,256]{1,0:T(8,128)(2,1)} %constant.27.clone.sel_ref) | copy-start | bytes 393220
  11.9 6.1 %copy-start.2 = (bf16[192,120]{1,0:T(8,128)(2,1)S(1)}, bf16[192,120]{1,0:T(8,128)(2,1)}, u32[]{:S(2)}) copy-start(bf16[192,120]{1,0:T(8,128)(2,1)} %constant.26.clone.order_ref) | copy-start | bytes 138244
  11.9 6.1 %copy-start.3 = (s32[8,2,512]{2,1,0:T(2,128)S(1)}, s32[8,2,512]{2,1,0:T(2,128)}, u32[]{:S(2)}) copy-start(s32[8,2,512]{2,1,0:T(2,128)} %cloud_ref.1) | copy-start | bytes 98308
  18.0 36.3 %copy-start.1 = (bf16[4,64,128]{2,1,0:T(8,128)(2,1)S(1)}, bf16[4,64,128]{2,1,0:T(8,128)(2,1)}, u32[]{:S(2)}) copy-start(bf16[4,64,128]{2,1,0:T(8,128)(2,1)} %param.26) | copy-start | bytes 196612
  54.3 0.7 copy-start.5

commit v5 on v4

--- a/solution.py
+++ b/solution.py
@@ -163,7 +163,9 @@
                 s1[base + fine_ch * v:base + fine_ch * (v + 1), :] = x.astype(BF)
     fines = []
     for g in range(4):
-        y = dot(w2_ref[...], s1[8 * fine_ch * g:8 * fine_ch * g + 16 * fine_ch, :])
+        w = w2_ref[:2 * fine_ch, :12 * fine_ch]
+        at = 8 * fine_ch * g
+        y = jnp.concatenate([dot(w, s1[at + 4 * fine_ch * k:at + 4 * fine_ch * (k + 3), :]) for k in range(2)], axis=0)
         f = act(y.reshape(4, fine_ch, half)).reshape(4 * fine_ch, half).astype(BF)
         if g in (1, 2):
             fines.append(f)

time: 77.6 us -> 74.9 us (0.965)
  Pallas kernels: 58.7 us -> 56.1 us
    pallas_call x1, Pallas kernels: 36.3 us -> 33.7 us  [body(): pl.pallas_call(functools.partial(encode_kernel, heads, fine_ch, coarse_ch...]
where the time goes in v5:
time: 74.9 us; the launch traced here: 74.6 us
  Pallas kernels  56.1 us (75%)
  starting transfers between devices  6.52 us (9%)
  local copies, waits for them, and re-layouts  6.12 us (8%)
  waiting for transfers between devices  5.11 us (7%)
    pallas_call x1, Pallas kernels, body(): pl.pallas_call(functools.partial(encode_kernel, heads, fine_ch, coarse_ch...  33.7 us
    pallas_call x1, Pallas kernels, body(): pl.pallas_call(functools.partial(tail_kernel, heads, fine_ch, coarse_ch,...  21.5 us
    ppermute x2, starting transfers between devices, neighbour_shift(): return lax.ppermute(x, ROWS, pairs)  6.52 us
    ppermute x2, waiting for transfers between devices, neighbour_shift(): return lax.ppermute(x, ROWS, pairs)  5.11 us
    unnamed x33, local copies, waits for them, and re-layouts  3.94 us
  transfers between devices with their start and end apart: 2, of which 2 were waited for; matrix products, arithmetic and copies ran while one was open for 2% of the time, Pallas kernels for 1%

profile of v5, /device:TPU:1, one launch (start us, length us, event | category | flops | bytes accessed | tf_op | source)
XLA Modules:
  0.0 74.6 jit_solution(6933037743278248109)
XLA Ops:
  0.0 1.5 %reshape.21.img_ref = bf16[8,40,1024]{2,1,0:T(8,128)(2,1)S(1)} reshape(bf16[8,10,4,1024]{3,2,1,0:T(4,128)(2,1)} %param.16) | data formatting | bytes 1310720 | tf_op jit(solution)/shard_map/reshape | solution.py:389
  1.5 4.6 %collective-permute-start = (bf16[8,40,1024]{2,1,0:T(8,128)(2,1)S(1)}, bf16[8,40,1024]{2,1,0:T(8,128)(2,1)S(1)}, u32[]{:S(2)}, u32[]{:S(2)}) collective-permute-start(bf16[8,40,1024]{2,1,0:T(8,128)(2,1)S(1)} %reshape.21.img_ref), channel_id=1, source_target_pairs={{0,1},{1,4},{4,5},{5,8},{8,9},{9,12},{12,13},{2,3},{3,6},{6,7},{7,... | collective-permute-start | bytes 1966088 | tf_op jit(solution)/shard_map/ppermute | solution.py:374
  6.1 1.9 %collective-permute-start.1 = (bf16[8,40,1024]{2,1,0:T(8,128)(2,1)S(1)}, bf16[8,40,1024]{2,1,0:T(8,128)(2,1)S(1)}, u32[]{:S(2)}, u32[]{:S(2)}) collective-permute-start(bf16[8,40,1024]{2,1,0:T(8,128)(2,1)S(1)} %reshape.21.img_ref), channel_id=1, source_target_pairs={{1,0},{4,1},{5,4},{8,5},{9,8},{12,9},{13,12},{3,2},{6,3},{7,6},{10... | collective-permute-start | bytes 1966088 | tf_op jit(solution)/shard_map/ppermute | solution.py:374
  8.1 0.2 copy.28.first_ref
  8.2 0.7 copy-done.10
  8.9 0.1 copy.29.down_ref
  9.1 0.6 copy-done.14
  9.7 0.1 multiply_sine_fusion
  9.8 0.2 fusion
  10.1 0.1 copy.31
  10.1 0.1 reshape.23
  10.3 0.2 copy.32.kb_ref
  10.5 0.3 copy-done.12
  10.8 0.1 reshape.24
  11.0 0.1 copy.33.q_ref
  11.1 0.7 copy-done.13
  11.8 0.1 copy.34.bias_ref
  11.9 0.9 %shard_map.154 = (bf16[256,256]{1,0:T(8,128)(2,1)S(1)}, bf16[256,1024]{1,0:T(8,128)(2,1)S(1)}, bf16[128,256]{1,0:T(8,128)(2,1)S(1)}, bf16[256,1536]{1,0:T(8,128)...) custom-call(bf16[9,64,10]{2,1,0:T(8,128)(2,1)S(1)} %copy.28.first_ref, ...), custom_call_target="tpu_custom_call" | custom-call | flops 1000000000 | bytes 6000000 | tf_op jit(solution)/shard_map/pallas_call | solution.py:413
  12.9 0.7 collective-permute-done.up_ref
  13.6 4.4 %collective-permute-done.1.dn_ref = bf16[8,40,1024]{2,1,0:T(8,128)(2,1)S(1)} collective-permute-done((bf16[8,40,1024]{2,1,0:T(8,128)(2,1)S(1)}, bf16[8,40,1024]{2,1,0:T(8,128)(2,1)S(1)}, u32[]{:S(2)}, u32[]{:S(2)}) %collective-permute-start.1) | collective-permute-done | bytes 655392 | tf_op jit(solution)/shard_map/ppermute | solution.py:374
  18.0 33.7 %shard_map.155 = (f32[32,512]{1,0:T(8,128)S(1)}, bf16[768,512]{1,0:T(8,128)(2,1)S(1)}) custom-call(f32[2]{0:T(128)S(1)} %add_convert_fusion.edge_ref, bf16[8,40,1024]{2,1,0:T(8,128)(2,1)S(1)} %collective-permute-done.up_ref, bf16[8,40,1024]{2,1,0:T(8,128)(2,1)S(1)} %reshape.21.img_ref, bf16[8,40,1024]{2,1,0:T(8,128)(2,1)S(1)} %collective-permute-done.1.dn_ref, ...), custom_call_target="tpu_custom_call" | custom-call | tf_op jit(solution)/shard_map/pallas_call | solution.py:434
  51.7 0.7 copy-done.5
  52.4 21.5 %shard_map.156 = f32[20,4,512]{2,1,0:T(4,128)S(1)} custom-call(f32[32,512]{1,0:T(8,128)S(1)} %get-tuple-element.19.ml_ref, bf16[768,512]{1,0:T(8,128)(2,1)S(1)} %get-tuple-element.20.ab_ref, bf16[128,128]{1,0:T(8,128)(2,1)S(1)} %get-tuple-element.21.wo_ref, bf16[256,128]{1,0:T(8,128)(2,1)S(1)} %bitcast.13, bf16[256,2048]{1,0:T(8,128)(2,1)S(1)} %get-tuple-element.22.wdec_ref, ...), custom_call_target="tpu_custom_call" | custom-call | tf_op jit(solution)/shard_map/pallas_call | solution.py:473
  73.9 0.7 copy.37
  (30 shorter events, 0.3 us)
Async XLA Ops:
  0.0 8.1 %copy-start.11 = (bf16[9,64,10]{1,2,0:T(8,128)(2,1)S(1)}, bf16[9,64,10]{1,2,0:T(8,128)(2,1)}, u32[]{:S(2)}) copy-start(bf16[9,64,10]{1,2,0:T(8,128)(2,1)} %param.19) | copy-start | bytes 34564
  1.5 12.1 %collective-permute-start = (bf16[8,40,1024]{2,1,0:T(8,128)(2,1)S(1)}, bf16[8,40,1024]{2,1,0:T(8,128)(2,1)S(1)}, u32[]{:S(2)}, u32[]{:S(2)}) collective-permute-start(bf16[8,40,1024]{2,1,0:T(8,128)(2,1)S(1)} %reshape.21.img_ref), channel_id=1, source_target_pairs={{0,1},{1,4},{4,5},{5,8},{8,9},{9,12},{12,13},{2,3},{3,6},{6,7},{7,... | collective-permute-start | bytes 1966088 | tf_op jit(solution)/shard_map/ppermute | solution.py:374
  6.1 11.9 %collective-permute-start.1 = (bf16[8,40,1024]{2,1,0:T(8,128)(2,1)S(1)}, bf16[8,40,1024]{2,1,0:T(8,128)(2,1)S(1)}, u32[]{:S(2)}, u32[]{:S(2)}) collective-permute-start(bf16[8,40,1024]{2,1,0:T(8,128)(2,1)S(1)} %reshape.21.img_ref), channel_id=1, source_target_pairs={{1,0},{4,1},{5,4},{8,5},{9,8},{12,9},{13,12},{3,2},{6,3},{7,6},{10... | collective-permute-start | bytes 1966088 | tf_op jit(solution)/shard_map/ppermute | solution.py:374
  8.1 0.8 %copy-start.10 = (bf16[4,128,64]{1,2,0:T(8,128)(2,1)S(1)}, bf16[4,128,64]{1,2,0:T(8,128)(2,1)}, u32[]{:S(2)}) copy-start(bf16[4,128,64]{1,2,0:T(8,128)(2,1)} %param.21) | copy-start | bytes 196612
  9.0 0.8 %copy-start.4 = (bf16[64,128]{1,0:T(8,128)(2,1)S(1)}, bf16[64,128]{1,0:T(8,128)(2,1)}, u32[]{:S(2)}) copy-start(bf16[64,128]{1,0:T(8,128)(2,1)} %key_ref.1) | copy-start | bytes 49156
  9.1 0.7 copy-start.14
  10.1 0.7 copy-start.12
  10.1 1.7 %copy-start.9 = (bf16[128,128]{1,0:T(8,128)(2,1)S(1)}, bf16[128,128]{1,0:T(8,128)(2,1)}, u32[]{:S(2)}) copy-start(bf16[128,128]{1,0:T(8,128)(2,1)} %out_ref.1) | copy-start | bytes 98308
  10.3 1.6 %copy-start.6 = (bf16[9,128,128]{2,1,0:T(8,128)(2,1)S(1)}, bf16[9,128,128]{2,1,0:T(8,128)(2,1)}, u32[]{:S(2)}) copy-start(bf16[9,128,128]{2,1,0:T(8,128)(2,1)} %coarse_ref.1) | copy-start | bytes 884740
  10.3 1.6 %copy-start.7 = (bf16[9,64,64]{2,1,0:T(8,128)(2,1)S(1)}, bf16[9,64,64]{2,1,0:T(8,128)(2,1)}, u32[]{:S(2)}) copy-start(bf16[9,64,64]{2,1,0:T(8,128)(2,1)} %second_ref.1) | copy-start | bytes 221188
  10.3 1.6 %copy-start.8 = (bf16[9,64,128]{2,1,0:T(8,128)(2,1)S(1)}, bf16[9,64,128]{2,1,0:T(8,128)(2,1)}, u32[]{:S(2)}) copy-start(bf16[9,64,128]{2,1,0:T(8,128)(2,1)} %dec_ref.1) | copy-start | bytes 442372
  11.1 0.7 copy-start.13
  11.9 6.1 %copy-start = (bf16[256,256]{1,0:T(8,128)(2,1)S(1)}, bf16[256,256]{1,0:T(8,128)(2,1)}, u32[]{:S(2)}) copy-start(bf16[256,256]{1,0:T(8,128)(2,1)} %constant.27.clone.sel_ref) | copy-start | bytes 393220
  11.9 6.1 %copy-start.2 = (bf16[192,120]{1,0:T(8,128)(2,1)S(1)}, bf16[192,120]{1,0:T(8,128)(2,1)}, u32[]{:S(2)}) copy-start(bf16[192,120]{1,0:T(8,128)(2,1)} %constant.26.clone.order_ref) | copy-start | bytes 138244
  11.9 6.1 %copy-start.3 = (s32[8,2,512]{2,1,0:T(2,128)S(1)}, s32[8,2,512]{2,1,0:T(2,128)}, u32[]{:S(2)}) copy-start(s32[8,2,512]{2,1,0:T(2,128)} %cloud_ref.1) | copy-start | bytes 98308
  18.0 33.7 %copy-start.1 = (bf16[4,64,128]{2,1,0:T(8,128)(2,1)S(1)}, bf16[4,64,128]{2,1,0:T(8,128)(2,1)}, u32[]{:S(2)}) copy-start(bf16[4,64,128]{2,1,0:T(8,128)(2,1)} %param.26) | copy-start | bytes 196612
  51.7 0.7 copy-start.5
